TPU v7x, 32 devices: a whole 2x2x4 slice. The times are simulated.
32 devices in a mesh: doc: 4 (over z), gram: 8 (over y, x, core).
Axes of the slice: x: 2, y: 2, z: 4, core: 2. Of those that a mesh axis runs over, the one named last changes fastest.
Arguments:
- w_factor: bfloat16 [6144, 256], P(('doc', 'gram')), may hold values from 0.003 to 0.1
- h_factor: bfloat16 [12288, 256], P(('gram', 'doc')), may hold values from 0.003 to 0.1
- tile_counts: bfloat16 [4, 8, 24, 128, 128], P('doc', 'gram'), may hold values from 0 to 30, as said below
- tile_rows: int32 [4, 8, 24], P('doc', 'gram'), may hold values from 0 to 11, as said below
- tile_cols: int32 [4, 8, 24], P('doc', 'gram'), may hold values from 0 to 11, as said below
- tile_live: int32 [4, 8], P('doc', 'gram'), may hold values from 1 to 24, as said below
Outputs:
- w_next: bfloat16 [6144, 256], P(('doc', 'gram'))
- h_next: bfloat16 [12288, 256], P(('gram', 'doc'))
Inputs may be any that keep to these rules, and one draw needn't show every extreme that they name: `tile_rows`: within one device pair the first tile_live slots name distinct tiles; slots hold positions in every case. `tile_cols`: see tile_rows. `tile_live`: some device pair holds 24 tiles. `tile_counts`: whole numbers.
All inputs are finite; a program needn't handle non-finite values.
Results may differ from a plain program's by a relative error of at most 0.0021.
Values may be sent and summed in bfloat16 or wider, within the bound.
No kernel may reach another device: no remote copies, remote signals or barrier semaphores. Data moves between devices by JAX's collectives and lax.ppermute only.
A program may use at most 64 MiB of HBM per device.

v0:
```python
import jax
import jax.numpy as jnp
from jax import lax
from jax.sharding import PartitionSpec as P

GROUP = 8


def group_terms(w_tiles, h_tiles, rows, cols, counts, keep):
    wt = jnp.take(w_tiles, rows, axis=0)
    ht = jnp.take(h_tiles, cols, axis=0)
    model = jnp.einsum("spk,sqk->spq", wt, ht, preferred_element_type=jnp.float32)
    ratio = (counts.astype(jnp.float32) / model * keep[:, None, None]).astype(jnp.bfloat16)
    w_part = jnp.einsum("spq,sqk->spk", ratio, ht, preferred_element_type=jnp.float32)
    h_part = jnp.einsum("spq,spk->sqk", ratio, wt, preferred_element_type=jnp.float32)
    pick_r = (rows[:, None] == jnp.arange(w_tiles.shape[0], dtype=jnp.int32)[None, :]).astype(
        jnp.float32
    )
    pick_c = (cols[:, None] == jnp.arange(h_tiles.shape[0], dtype=jnp.int32)[None, :]).astype(
        jnp.float32
    )
    add_w = jnp.einsum("st,spk->tpk", pick_r, w_part, precision=lax.Precision.HIGHEST)
    add_h = jnp.einsum("st,spk->tpk", pick_c, h_part, precision=lax.Precision.HIGHEST)
    return (add_w, add_h)


def body(w_factor, h_factor, tile_counts, tile_rows, tile_cols, tile_live):
    topics = w_factor.shape[1]
    w_block = lax.all_gather(w_factor, "gram", axis=0, tiled=True)
    h_block = lax.all_gather(h_factor, "doc", axis=0, tiled=True)
    tile_side = tile_counts.shape[3]
    w_tiles = w_block.reshape(-1, tile_side, topics)
    h_tiles = h_block.reshape(-1, tile_side, topics)
    rows = tile_rows[0, 0]
    cols = tile_cols[0, 0]
    counts = tile_counts[0, 0]
    live = tile_live[0, 0]
    slots = rows.shape[0]
    width = GROUP
    start = (jnp.zeros(w_tiles.shape, jnp.float32), jnp.zeros(h_tiles.shape, jnp.float32))
    steps = slots // width
    marks = (jnp.arange(slots, dtype=jnp.int32) < live).astype(jnp.float32)

    def visit(carry, pieces):
        part_rows, part_cols, part_counts, part_keep = pieces
        add_w, add_h = group_terms(w_tiles, h_tiles, part_rows, part_cols, part_counts, part_keep)
        return ((carry[0] + add_w, carry[1] + add_h), None)

    pieces = (
        rows.reshape(steps, width),
        cols.reshape(steps, width),
        counts.reshape(steps, width, tile_side, tile_side),
        marks.reshape(steps, width),
    )
    (w_numer, h_numer), _ = lax.scan(visit, start, pieces)
    flat_w = w_numer.reshape(-1, topics)
    flat_h = h_numer.reshape(-1, topics)
    w_rows = w_factor.shape[0]
    h_rows = h_factor.shape[0]
    summed_w = lax.psum(flat_w, "gram")
    share_w = lax.dynamic_slice_in_dim(summed_w, lax.axis_index("gram") * w_rows, w_rows, 0)
    summed_h = lax.psum(flat_h, "doc")
    share_h = lax.dynamic_slice_in_dim(summed_h, lax.axis_index("doc") * h_rows, h_rows, 0)
    h_sums = jnp.sum(h_factor.astype(jnp.float32), axis=0)
    w_sums = jnp.sum(w_factor.astype(jnp.float32), axis=0)
    w_denom, h_denom = lax.psum((h_sums, w_sums), ("doc", "gram"))
    w_next = (w_factor.astype(jnp.float32) * share_w / w_denom).astype(jnp.bfloat16)
    h_next = (h_factor.astype(jnp.float32) * share_h / h_denom).astype(jnp.bfloat16)
    return (w_next, h_next)


def solution(mesh):
    in_specs = (
        P(("doc", "gram"), None),
        P(("gram", "doc"), None),
        P("doc", "gram", None, None, None),
        P("doc", "gram", None),
        P("doc", "gram", None),
        P("doc", "gram"),
    )
    out_specs = (P(("doc", "gram"), None), P(("gram", "doc"), None))
    return jax.shard_map(body, mesh=mesh, in_specs=in_specs, out_specs=out_specs, check_vma=False)
```

profile of v0, /device:TPU:0, one launch (start us, length us, event | category | flops | bytes accessed | tf_op | source)
XLA Modules:
  0.0 222.5 jit_solution(12849468486808547463)
XLA Ops:
  7.2 0.0 all-reduce.4.cloned.1.call-start
  7.2 0.5 broadcast.73
  7.7 1.3 reduce.6
  9.1 0.1 reshape_squeeze.9
  9.1 12.2 %all_gather.6 = bf16[1536,256]{1,0:T(8,128)(2,1)S(1)} all-gather(bf16[192,256]{1,0:T(8,128)(2,1)} %param.10), channel_id=1, replica_groups=mesh['doc'=4,'gram'=8] {'gram'}, dimensions={0}, use_global_device_ids=true | all-gather | bytes 884736 | tf_op jit(solution)/shard_map/all_gather | solution.py:29
  21.3 1.3 reduce.7
  22.7 0.1 reshape_squeeze.11
  22.7 20.4 %all_gather.7 = bf16[1536,256]{1,0:T(8,128)(2,1)} all-gather(bf16[384,256]{1,0:T(8,128)(2,1)} %param.11), channel_id=1, replica_groups=mesh['doc'=4,'gram'=8] {'doc'}, dimensions={0}, use_global_device_ids=true | all-gather | bytes 983040 | tf_op jit(solution)/shard_map/all_gather | solution.py:30
  43.8 38.7 %while.13 = (s32[]{:T(128)}, f32[12,128,256]{2,0,1:T(8,128)S(1)}, f32[12,128,256]{2,0,1:T(8,128)}, s32[3,8]{1,0:T(4,128)S(1)}, bf16[3,8,128,128]{3,2,1,0:T(8,128...) while((s32[]{:T(128)}, f32[12,128,256]{2,0,1:T(8,128)S(1)}, ...), condition=%wide.region_1.3_spmd.clone, body=%wide.region_0.2_spmd.clone.sunk | while | flops 279972160 | bytes 40903584 | solution.py:55
  43.8 0.0 copy-start.5
  43.9 0.6 gather_fusion
  44.5 0.0 copy-start.2
  44.5 0.2 copy-done.5
  44.7 1.7 gather_fusion.1
  46.4 0.0 copy-start.4
  46.4 0.8 copy-done.4
  47.2 1.3 fusion.44
  48.6 1.4 fusion.45
  50.0 2.5 %select_add_fusion.4 = f32[12,128,256]{2,0,1:T(8,128)S(1)} fusion(f32[12,128,256]{2,0,1:T(8,128)S(1)} %get-tuple-element.184, f32[8,128,256]{2,1,0:T(8,128)S(1)} %fusion.45, pred[]{:T(512)S(6)} %compare.3, s32[8]{0:T(128)S(1)} %get-tuple-element.168), kind=kOutput, calls=%fused_computation.3.clone.1 | convolution fusion | flops 38535264 | bytes 4194337 | tf_op jit(solution)/shard_map/while/body/eval_jaxpr/st,spk->tpk/dot_general | solution.py:22
  52.5 0.4 fusion.46
  52.9 2.5 %select_add_fusion.5 = f32[12,128,256]{2,0,1:T(8,128)S(1)} fusion(f32[12,128,256]{2,0,1:T(8,128)S(1)} %copy-done, f32[8,128,256]{2,1,0:T(8,128)S(1)} %fusion.46, pred[]{:T(512)S(6)} %compare.3, s32[8]{0:T(128)S(1)} %get-tuple-element.170), kind=kOutput, calls=%fused_computation.2.clone.1 | convolution fusion | flops 38535264 | bytes 4194337 | tf_op jit(solution)/shard_map/while/body/eval_jaxpr/st,spk->tpk/dot_general | solution.py:23
  55.4 1.3 copy-done.1
  56.7 0.0 copy-done.6
  56.8 0.6 gather_fusion
  57.4 0.2 copy-done.5
  57.6 1.7 gather_fusion.1
  59.3 0.0 copy-start.4
  59.3 0.0 copy-done.2
  59.3 0.8 copy-done.4
  60.1 1.3 fusion.44
  61.5 1.4 fusion.45
  62.9 0.0 copy-start.3
  62.9 0.0 copy-start
  62.9 2.5 %select_add_fusion.4 = f32[12,128,256]{2,0,1:T(8,128)S(1)} fusion(f32[12,128,256]{2,0,1:T(8,128)S(1)} %get-tuple-element.184, f32[8,128,256]{2,1,0:T(8,128)S(1)} %fusion.45, pred[]{:T(512)S(6)} %compare.3, s32[8]{0:T(128)S(1)} %get-tuple-element.168), kind=kOutput, calls=%fused_computation.3.clone.1 | convolution fusion | flops 38535264 | bytes 4194337 | tf_op jit(solution)/shard_map/while/body/eval_jaxpr/st,spk->tpk/dot_general | solution.py:22
  65.4 0.4 fusion.46
  65.8 0.0 copy-done
  65.8 0.0 copy-start.6
  65.8 2.5 %select_add_fusion.5 = f32[12,128,256]{2,0,1:T(8,128)S(1)} fusion(f32[12,128,256]{2,0,1:T(8,128)S(1)} %copy-done, f32[8,128,256]{2,1,0:T(8,128)S(1)} %fusion.46, pred[]{:T(512)S(6)} %compare.3, s32[8]{0:T(128)S(1)} %get-tuple-element.170), kind=kOutput, calls=%fused_computation.2.clone.1 | convolution fusion | flops 38535264 | bytes 4194337 | tf_op jit(solution)/shard_map/while/body/eval_jaxpr/st,spk->tpk/dot_general | solution.py:23
  68.3 1.3 copy-done.1
  69.7 0.6 gather_fusion
  70.3 0.2 copy-done.5
  70.5 1.7 gather_fusion.1
  72.2 0.8 copy-done.4
  73.0 1.3 fusion.44
  74.4 1.4 fusion.45
  75.8 2.5 %select_add_fusion.4 = f32[12,128,256]{2,0,1:T(8,128)S(1)} fusion(f32[12,128,256]{2,0,1:T(8,128)S(1)} %get-tuple-element.184, f32[8,128,256]{2,1,0:T(8,128)S(1)} %fusion.45, pred[]{:T(512)S(6)} %compare.3, s32[8]{0:T(128)S(1)} %get-tuple-element.168), kind=kOutput, calls=%fused_computation.3.clone.1 | convolution fusion | flops 38535264 | bytes 4194337 | tf_op jit(solution)/shard_map/while/body/eval_jaxpr/st,spk->tpk/dot_general | solution.py:22
  78.3 0.4 fusion.46
  78.7 2.5 %select_add_fusion.5 = f32[12,128,256]{2,0,1:T(8,128)S(1)} fusion(f32[12,128,256]{2,0,1:T(8,128)S(1)} %copy-done, f32[8,128,256]{2,1,0:T(8,128)S(1)} %fusion.46, pred[]{:T(512)S(6)} %compare.3, s32[8]{0:T(128)S(1)} %get-tuple-element.170), kind=kOutput, calls=%fused_computation.2.clone.1 | convolution fusion | flops 38535264 | bytes 4194337 | tf_op jit(solution)/shard_map/while/body/eval_jaxpr/st,spk->tpk/dot_general | solution.py:23
  81.2 0.0 copy-start.1
  81.2 1.3 copy-done.1
  82.5 2.1 copy.8
  84.6 0.0 all-reduce.4.cloned.1.call-update
  84.6 0.0 all-reduce.6.cloned.1.call-start
  84.7 0.0 copy-start.8
  84.7 0.0 copy-start.7
  84.7 3.8 %copy.9 = f32[12,128,256]{2,1,0:T(8,128)} copy(f32[12,128,256]{2,0,1:T(8,128)} %get-tuple-element.52) | data formatting | bytes 3145728 | tf_op jit(solution)/shard_map/while | solution.py:55
  88.5 0.0 all-reduce.6.cloned.1.call-update
  88.5 0.0 copy-done.8
  88.6 0.1 convert_reduce_fusion
  88.6 37.9 %all-reduce = (f32[256]{0:T(256)S(1)}, f32[256]{0:T(256)S(1)}) all-reduce(f32[256]{0:T(256)S(1)} %convert_reduce_fusion, f32[256]{0:T(256)S(1)} %convert_reduce_fusion.1), channel_id=1, replica_groups=mesh['doc'=4,'gram'=8] {'doc','gram'}, use_global_device_ids=true, to_apply=%region_4.6 | all-reduce | flops 512 | bytes 4096 | tf_op jit(solution)/shard_map/psum | solution.py:66
  126.5 16.4 %all-reduce.4.cloned.1.call-done = f32[1536,256]{1,0:T(8,128)} async-done(((f32[1536,256]{1,0:T(8,128)}), f32[1536,256]{1,0:T(8,128)}) %all-reduce.4.cloned.1.call-update) | async-done | bytes 1572880 | tf_op jit(solution)/shard_map/psum | solution.py:60
  142.9 1.6 fusion.21
  144.5 69.4 %all-reduce.6.cloned.1.call-done = f32[1536,256]{1,0:T(8,128)} async-done(((f32[1536,256]{1,0:T(8,128)}), f32[1536,256]{1,0:T(8,128)}) %all-reduce.6.cloned.1.call-update) | async-done | bytes 1572880 | tf_op jit(solution)/shard_map/psum | solution.py:62
  213.9 1.7 fusion.19
  (45 shorter events, 0.2 us)
Async XLA Ops:
  7.2 135.8 %all-reduce.4.cloned.1.call-start = ((), (), s32[]{:S(2)}) async-start(), calls=%async_computation | async-start | bytes 3145728 | tf_op jit(solution)/shard_map/psum | solution.py:60
  43.8 0.9 copy-start.5
  44.5 2.0 copy-start.2
  46.4 0.8 copy-start.4
  50.0 2.5 %copy-start.3 = (bf16[8,128,256]{2,1,0:T(8,128)(2,1)S(1)}, bf16[8,128,256]{2,1,0:T(8,128)(2,1)}, u32[]{:S(2)}) copy-start(bf16[8,128,256]{2,1,0:T(8,128)(2,1)} %copy-done.2) | copy-start | bytes 1572868 | tf_op jit(solution)/shard_map/while
  50.0 2.9 %copy-start = (f32[12,128,256]{2,0,1:T(8,128)S(1)}, f32[12,128,256]{2,0,1:T(8,128)}, u32[]{:S(2)}) copy-start(f32[12,128,256]{2,0,1:T(8,128)} %get-tuple-element.185) | copy-start | bytes 4718596 | tf_op jit(solution)/shard_map/while
  52.9 3.8 %copy-start.6 = (bf16[12,128,256]{2,1,0:T(8,128)(2,1)S(1)}, bf16[12,128,256]{2,1,0:T(8,128)(2,1)}, u32[]{:S(2)}) copy-start(bf16[12,128,256]{2,1,0:T(8,128)(2,1)} %copy-done.5) | copy-start | bytes 2359300 | tf_op jit(solution)/shard_map/while
  55.4 1.4 copy-start.1
  56.7 0.9 copy-start.5
  57.4 2.0 copy-start.2
  59.3 0.8 copy-start.4
  62.9 2.5 %copy-start.3 = (bf16[8,128,256]{2,1,0:T(8,128)(2,1)S(1)}, bf16[8,128,256]{2,1,0:T(8,128)(2,1)}, u32[]{:S(2)}) copy-start(bf16[8,128,256]{2,1,0:T(8,128)(2,1)} %copy-done.2) | copy-start | bytes 1572868 | tf_op jit(solution)/shard_map/while
  62.9 2.9 %copy-start = (f32[12,128,256]{2,0,1:T(8,128)S(1)}, f32[12,128,256]{2,0,1:T(8,128)}, u32[]{:S(2)}) copy-start(f32[12,128,256]{2,0,1:T(8,128)} %get-tuple-element.185) | copy-start | bytes 4718596 | tf_op jit(solution)/shard_map/while
  65.8 3.8 %copy-start.6 = (bf16[12,128,256]{2,1,0:T(8,128)(2,1)S(1)}, bf16[12,128,256]{2,1,0:T(8,128)(2,1)}, u32[]{:S(2)}) copy-start(bf16[12,128,256]{2,1,0:T(8,128)(2,1)} %copy-done.5) | copy-start | bytes 2359300 | tf_op jit(solution)/shard_map/while
  68.3 1.4 copy-start.1
  69.6 0.9 copy-start.5
  70.3 2.0 copy-start.2
  72.2 0.8 copy-start.4
  75.8 2.5 %copy-start.3 = (bf16[8,128,256]{2,1,0:T(8,128)(2,1)S(1)}, bf16[8,128,256]{2,1,0:T(8,128)(2,1)}, u32[]{:S(2)}) copy-start(bf16[8,128,256]{2,1,0:T(8,128)(2,1)} %copy-done.2) | copy-start | bytes 1572868 | tf_op jit(solution)/shard_map/while
  75.8 2.9 %copy-start = (f32[12,128,256]{2,0,1:T(8,128)S(1)}, f32[12,128,256]{2,0,1:T(8,128)}, u32[]{:S(2)}) copy-start(f32[12,128,256]{2,0,1:T(8,128)} %get-tuple-element.185) | copy-start | bytes 4718596 | tf_op jit(solution)/shard_map/while
  78.7 3.8 %copy-start.6 = (bf16[12,128,256]{2,1,0:T(8,128)(2,1)S(1)}, bf16[12,128,256]{2,1,0:T(8,128)(2,1)}, u32[]{:S(2)}) copy-start(bf16[12,128,256]{2,1,0:T(8,128)(2,1)} %copy-done.5) | copy-start | bytes 2359300 | tf_op jit(solution)/shard_map/while
  81.2 1.4 copy-start.1
  84.6 129.3 %all-reduce.6.cloned.1.call-start = ((), (), s32[]{:S(2)}) async-start(), calls=%async_computation.1 | async-start | bytes 3145728 | tf_op jit(solution)/shard_map/psum | solution.py:62
  84.7 3.8 %copy-start.8 = (bf16[192,256]{1,0:T(8,128)(2,1)S(1)}, bf16[192,256]{1,0:T(8,128)(2,1)}, u32[]{:S(2)}) copy-start(bf16[192,256]{1,0:T(8,128)(2,1)} %param.10) | copy-start | bytes 294916
  84.7 3.9 %copy-start.7 = (bf16[384,256]{1,0:T(8,128)(2,1)S(1)}, bf16[384,256]{1,0:T(8,128)(2,1)}, u32[]{:S(2)}) copy-start(bf16[384,256]{1,0:T(8,128)(2,1)} %param.11) | copy-start | bytes 589828
Sparse Core Ops, SparseCore 0:
  84.8 58.1 all-reduce.3
  145.4 68.4 all-reduce.5
where the time goes:
time: 223 us; the launch traced here: 222 us
  waiting for transfers between devices  85.8 us (38%)
  blocking collectives  70.5 us (32%)
  matrix products  24.2 us (11%)
  local copies, waits for them, and re-layouts  20.5 us (9%)
  between operations  14.8 us (7%)
  other arithmetic  6.18 us (3%)
    psum x1, waiting for transfers between devices, body(): summed_h = lax.psum(flat_h, 'doc')  69.4 us
    psum x1, blocking collectives, body(): w_denom, h_denom = lax.psum((h_sums, w_sums), ('doc', 'gram'))  37.9 us
    all_gather x1, blocking collectives, body(): h_block = lax.all_gather(h_factor, 'doc', axis=0, tiled=True)  20.4 us
    psum x1, waiting for transfers between devices, body(): summed_w = lax.psum(flat_w, 'gram')  16.4 us
    all_gather x1, blocking collectives, body(): w_block = lax.all_gather(w_factor, 'gram', axis=0, tiled=True)  12.2 us
    dot_general x3, matrix products, group_terms(): jnp.einsum('st,spk->tpk', pick_c, h_part, precision=lax.Precision.HIGHEST)  7.43 us
    dot_general x3, matrix products, group_terms(): jnp.einsum('st,spk->tpk', pick_r, w_part, precision=lax.Precision.HIGHEST)  7.43 us
    while x42, local copies, waits for them, and re-layouts  7.03 us
  transfers between devices with their start and end apart: 2, of which 2 were waited for; matrix products, arithmetic and copies ran while one was open for 2% of the time, Pallas kernels for 0%

commit v1 on v0

v1 whole, which is shorter than its diff:
```python
import functools

import jax
import jax.numpy as jnp
from jax import lax
from jax.experimental import pallas as pl
from jax.experimental.pallas import tpu as pltpu
from jax.sharding import PartitionSpec as P

OUTER = 4
EXTRA = 8
STEP_RATIO = 8
STEP_SUM = 4
SCALE = 2.0**-5
FIRST_GROUP = (3,)
LAST_GROUP = (0, 1, 2)


def partner(outer, inner, by_outer, by_inner):
    return [
        ((o * inner + i), (o ^ by_outer) * inner + (i ^ by_inner))
        for o in range(outer)
        for i in range(inner)
    ]


def partial_sums(block):
    rows, k = block.shape
    return jnp.sum(block.astype(jnp.float32).reshape(rows // EXTRA, EXTRA, k), axis=0)


def visit_tiles(
    group, side, w_ref, counts, acc, h_outs, order, ratios, h_all, h_sum, rows, cols, live
):
    quarter = h_all.shape[0] // len(group)
    me_h = lax.axis_index("doc") // (lax.axis_size("doc") // OUTER)

    def quarter_of(slot):
        return (cols[0, 0, slot] * side) // quarter ^ me_h

    def scan(slot, found):
        near = quarter_of(slot)
        hit = near == group[0]
        for member in group[1:]:
            hit = hit | (near == member)
        order[found] = slot
        return found + jnp.where(hit, 1, 0)

    found = lax.fori_loop(0, live[0, 0], scan, 0)
    for extra in range(max(STEP_RATIO, STEP_SUM)):
        order[found + extra] = 0

    def tile_at(j):
        slot = order[j]
        near = quarter_of(slot)
        at = jnp.int32(0)
        for k, member in enumerate(group):
            at = jnp.where(near == member, k, at)
        row = pl.multiple_of(rows[0, 0, slot] * side, side)
        col = at * quarter + lax.rem(cols[0, 0, slot] * side, quarter)
        return slot, row, pl.multiple_of(col, side)

    def make_ratios(step, carry):
        made = []
        for k in range(STEP_RATIO):
            j = step * STEP_RATIO + k
            slot, row, col = tile_at(j)
            model = lax.dot_general(
                w_ref[pl.ds(row, side), :],
                h_all[pl.ds(col, side), :],
                (((1,), (1,)), ((), ())),
                preferred_element_type=jnp.float32,
            )
            keep = jnp.where(j < found, 1.0, 0.0)
            made.append((counts[slot].astype(jnp.float32) / model * keep).astype(jnp.bfloat16))
        for k, ratio in enumerate(made):
            ratios[step * STEP_RATIO + k] = ratio
        return carry

    def add_terms(step, carry):
        terms = []
        for k in range(STEP_SUM):
            j = step * STEP_SUM + k
            slot, row, col = tile_at(j)
            ratio = ratios[j]
            w_part = jnp.dot(
                ratio, h_all[pl.ds(col, side), :], preferred_element_type=jnp.float32
            )
            h_part = lax.dot_general(
                ratio,
                w_ref[pl.ds(row, side), :],
                (((0,), (0,)), ((), ())),
                preferred_element_type=jnp.float32,
            )
            terms.append((row, col, w_part, h_part))
        for row, col, w_part, h_part in terms:
            acc[pl.ds(row, side), :] += w_part
            h_sum[pl.ds(col, side), :] += h_part
        return carry

    lax.fori_loop(0, (found + STEP_RATIO - 1) // STEP_RATIO, make_ratios, 0)
    lax.fori_loop(0, (found + STEP_SUM - 1) // STEP_SUM, add_terms, 0)

    w_sums = partial_sums(w_ref[...])
    for at, h_out in enumerate(h_outs):
        h_out[:quarter, :] = h_sum[at * quarter : (at + 1) * quarter, :]
        h_out[quarter:, :] = w_sums


def started(sems, *pairs):
    copies = [
        pltpu.make_async_copy(source, target, sems.at[k])
        for k, (source, target) in enumerate(pairs)
    ]
    for copy in copies:
        copy.start()
    return copies


def first_kernel(group, side, inner, rows_in, cols_in, live, stored, w_block, *refs):
    h_pieces, refs = refs[: len(group)], refs[len(group) :]
    acc, counts, refs = refs[0], refs[1], refs[2:]
    h_outs, refs = refs[: len(group)], refs[len(group) :]
    sems, order, ratios, h_all, h_sum, rows, cols = refs
    copies = started(sems, (rows_in, rows), (cols_in, cols), (stored.at[0, 0], counts))
    quarter = h_pieces[0].shape[0]
    w_len = w_block.shape[0]
    for at, piece in enumerate(h_pieces):
        h_all[at * quarter : (at + 1) * quarter, :] = piece[...]
    acc[:w_len, :] = jnp.zeros((w_len, acc.shape[1]), jnp.float32)
    acc[w_len:, :] = partial_sums(h_all[...])
    h_sum[...] = jnp.zeros_like(h_sum)
    for copy in copies:
        copy.wait()
    visit_tiles(
        group, side, w_block, counts, acc, h_outs, order, ratios, h_all, h_sum, rows, cols, live
    )


def last_kernel(group, side, inner, rows_in, cols_in, live, counts, w_block, acc_in, *refs):
    mine, h_pieces, refs = refs[0], refs[1 : len(group)], refs[len(group) :]
    w_outs, refs = refs[:inner], refs[inner:]
    h_outs, refs = refs[: len(group)], refs[len(group) :]
    sems, order, ratios, h_all, h_sum, rows, cols, acc = refs
    quarter = mine.shape[0]
    copies = started(
        sems, (rows_in, rows), (cols_in, cols), (mine, h_all.at[pl.ds(0, quarter)])
    )
    w_len = w_block.shape[0]
    w_rows = w_len // (inner * OUTER)
    for at, piece in enumerate(h_pieces):
        h_all[(at + 1) * quarter : (at + 2) * quarter, :] = piece[...]
    acc[:w_len, :] = acc_in[:w_len, :]
    h_sum[...] = jnp.zeros_like(h_sum)
    for copy in copies:
        copy.wait()
    acc[w_len:, :] = acc_in[w_len:, :] + partial_sums(h_all[...])
    visit_tiles(
        group, side, w_block, counts, acc, h_outs, order, ratios, h_all, h_sum, rows, cols, live
    )
    me_w = lax.axis_index("gram")
    me_o, me_i = me_w // inner, lax.rem(me_w, inner)
    for i in range(inner):
        for o in range(OUTER):
            at = pl.multiple_of(((me_o ^ o) * inner + (me_i ^ i)) * w_rows, 8)
            w_outs[i][o, :w_rows, :] = acc[pl.ds(at, w_rows), :]
            w_outs[i][o, w_rows:, :] = acc[w_len:, :]


def in_hbm(x):
    return pltpu.with_memory_space_constraint(x, pltpu.HBM)


def run_kernel(kernel, group, inner, args, from_hbm, out_shapes, quarter, acc_shape):
    rows, cols, _, counts = args[:4]
    slots, side = counts.shape[-3:-1]
    topics = acc_shape[1]
    width = len(group)
    pad = max(STEP_RATIO, STEP_SUM)
    scratch = [
        pltpu.SemaphoreType.DMA((3,)),
        pltpu.SMEM((slots + pad,), jnp.int32),
        pltpu.VMEM((slots + pad, side, side), jnp.bfloat16),
        pltpu.VMEM((width * quarter, topics), jnp.bfloat16),
        pltpu.VMEM((width * quarter, topics), jnp.float32),
        pltpu.SMEM(rows.shape, rows.dtype),
        pltpu.SMEM(cols.shape, cols.dtype),
    ]
    if kernel is last_kernel:
        scratch.append(pltpu.VMEM(acc_shape, jnp.float32))
    spaces = [pltpu.HBM if at in from_hbm else pltpu.VMEM for at in range(len(args))]
    spaces[2] = pltpu.SMEM
    args = [in_hbm(x) if at in from_hbm else x for at, x in enumerate(args)]
    return pl.pallas_call(
        functools.partial(kernel, group, side, inner),
        out_shape=out_shapes,
        in_specs=[pl.BlockSpec(memory_space=space) for space in spaces],
        out_specs=[pl.BlockSpec(memory_space=pltpu.VMEM)] * len(out_shapes),
        scratch_shapes=scratch,
        compiler_params=pltpu.CompilerParams(vmem_limit_bytes=32 * 1024 * 1024),
        cost_estimate=pl.CostEstimate(
            flops=36 * width * side * side * topics, bytes_accessed=1 << 23, transcendentals=0
        ),
    )(*args)


def body(w_factor, h_factor, tile_counts, tile_rows, tile_cols, tile_live):
    doc, gram = lax.axis_size("doc"), lax.axis_size("gram")
    inner_h, inner_w = doc // OUTER, gram // OUTER
    w_rows, topics = w_factor.shape
    h_rows = h_factor.shape[0]
    w_len = w_rows * gram

    def send_h(x, by_outer, by_inner=0):
        return lax.ppermute(x, "doc", partner(OUTER, inner_h, by_outer, by_inner))

    def send_w(x, by_outer, by_inner=0):
        return lax.ppermute(x, "gram", partner(OUTER, inner_w, by_outer, by_inner))

    if inner_h > 1:
        ring = [[o * inner_h + i for i in range(inner_h)] for o in range(OUTER)]
        mine = lax.all_gather(h_factor, "doc", axis=0, tiled=True, axis_index_groups=ring)
    else:
        mine = h_factor
    quarter = mine.shape[0]
    h_pieces = {0: mine}
    for m in (3, 2, 1):
        h_pieces[m] = send_h(mine, m)
    w_block = lax.all_gather(w_factor, "gram", axis=0, tiled=True)

    places = [tile_rows, tile_cols, tile_live]
    acc_shape = jax.ShapeDtypeStruct((w_len + EXTRA, topics), jnp.float32)
    h_shape = jax.ShapeDtypeStruct((quarter + EXTRA, topics), jnp.float32)
    w_shape = jax.ShapeDtypeStruct((OUTER, w_rows + EXTRA, topics), jnp.float32)
    acc, counts, far = run_kernel(
        first_kernel,
        FIRST_GROUP,
        inner_w,
        [*places, tile_counts, w_block, *[h_pieces[m] for m in FIRST_GROUP]],
        (0, 1, 3),
        [acc_shape, jax.ShapeDtypeStruct(tile_counts.shape[2:], tile_counts.dtype), h_shape],
        quarter,
        acc_shape.shape,
    )
    h_scale = SCALE / 2
    far = send_h((far * h_scale).astype(jnp.float16), 1)
    outs = run_kernel(
        last_kernel,
        LAST_GROUP,
        inner_w,
        [*places, counts, w_block, acc, *[h_pieces[m] for m in LAST_GROUP]],
        (0, 1, 6),
        [w_shape] * inner_w + [h_shape] * len(LAST_GROUP),
        quarter,
        acc_shape.shape,
    )
    far, *w_outs = lax.optimization_barrier((far, *outs[:inner_w]))
    terms = dict(zip(LAST_GROUP, outs[inner_w:]))
    across = (terms[2] * h_scale + far.astype(jnp.float32)).astype(jnp.float16)
    across = send_h(across, 2)

    w_scale = SCALE / inner_w
    w_got = [send_w(w_outs[i], 0, i) for i in range(1, inner_w)]
    near, *w_got = lax.optimization_barrier(((terms[1] * h_scale).astype(jnp.float16), *w_got))
    near = send_h(near, 1)
    w_terms = w_outs[0]
    for got in w_got:
        w_terms = w_terms + got
    w_sent = [
        send_w((w_terms[o] * w_scale).astype(jnp.float16), o) for o in range(1, OUTER)
    ]

    h_total = terms[0] * h_scale + across.astype(jnp.float32) + near.astype(jnp.float32)
    if inner_h > 1:
        me_i = lax.rem(lax.axis_index("doc"), inner_h)
        tail = h_total[-EXTRA:]

        def share(i):
            part = lax.dynamic_slice_in_dim(h_total, (me_i ^ i) * h_rows, h_rows, 0)
            return jnp.concatenate([part, tail], axis=0)

        total = share(0)
        for i in range(1, inner_h):
            total = total + send_h(share(i), 0, i)
        h_total = total
    h_denom = jnp.sum(h_total[h_rows:], axis=0)
    h_next = (h_factor.astype(jnp.float32) * h_total[:h_rows] / h_denom).astype(jnp.bfloat16)

    h_next, *w_sent = lax.optimization_barrier((h_next, *w_sent))
    w_total = w_terms[0] * w_scale
    for got in w_sent:
        w_total = w_total + got.astype(jnp.float32)
    w_denom = jnp.sum(w_total[w_rows:], axis=0)
    w_next = (w_factor.astype(jnp.float32) * w_total[:w_rows] / w_denom).astype(jnp.bfloat16)
    return (w_next, h_next)


def solution(mesh):
    in_specs = (
        P(("doc", "gram"), None),
        P(("gram", "doc"), None),
        P("doc", "gram", None, None, None),
        P("doc", "gram", None),
        P("doc", "gram", None),
        P("doc", "gram"),
    )
    out_specs = (P(("doc", "gram"), None), P(("gram", "doc"), None))
    return jax.shard_map(body, mesh=mesh, in_specs=in_specs, out_specs=out_specs, check_vma=False)
```

time: 223 us -> 42.8 us (0.19)
  waiting for transfers between devices: 85.8 us -> 8.61 us
  blocking collectives: 70.5 us -> 10.9 us
  matrix products: 24.2 us -> 0 us
  local copies, waits for them, and re-layouts: 20.5 us -> 0.01 us
  starting transfers between devices: 0.08 us -> 16.3 us
  between operations: 14.8 us -> 1.36 us
  other arithmetic: 6.18 us -> 1.96 us
  Pallas kernels: 0 us -> 4.04 us
    psum x2 -> x0, waiting for transfers between devices: 85.8 us -> none  [the longest x1 69.4 us: body(): summed_h = lax.psum(flat_h, 'doc')]
    psum x1 -> x0, blocking collectives: 37.9 us -> none  [body(): w_denom, h_denom = lax.psum((h_sums, w_sums), ('doc', 'gram'))]
    dot_general x15 -> x0, matrix products: 24.2 us -> none  [the longest x3 7.43 us: group_terms(): jnp.einsum('st,spk->tpk', pick_c, h_part, precision=lax.Precision.HIGHEST)]
    all_gather x1 -> x0, blocking collectives: 20.4 us -> none  [body(): h_block = lax.all_gather(h_factor, 'doc', axis=0, tiled=True)]
    ppermute x0 -> x10, starting transfers between devices: none -> 16.3 us  [the longest x6 12.7 us: send_h(): return lax.ppermute(x, 'doc', partner(OUTER, inner_h, by_outer, by_inner))]
    while x44 -> x0, local copies, waits for them, and re-layouts: 12.9 us -> none
    ppermute x0 -> x10, waiting for transfers between devices: none -> 8.61 us  [the longest x6 8.6 us: send_h(): return lax.ppermute(x, 'doc', partner(OUTER, inner_h, by_outer, by_inner))]
    gather x6 -> x0, local copies, waits for them, and re-layouts: 6.87 us -> none  [the longest x3 5.13 us: group_terms(): ht = jnp.take(h_tiles, cols, axis=0)]
  transfers between devices with their start and end apart: 2 -> 10, of which waited for: 2 -> 4; matrix products, arithmetic and copies ran while one was open for 2% -> 3% of each run, Pallas kernels for 0% -> 9%
where the time goes in v1:
time: 42.8 us; the launch traced here: 43.1 us
  starting transfers between devices  16.3 us (38%)
  blocking collectives  10.9 us (25%)
  waiting for transfers between devices  8.61 us (20%)
  Pallas kernels  4.04 us (9%)
  other arithmetic  1.96 us (5%)
  between operations  1.36 us (3%)
    ppermute x6, starting transfers between devices, send_h(): return lax.ppermute(x, 'doc', partner(OUTER, inner_h, by_outer, by_inner))  12.7 us
    all_gather x1, blocking collectives, body(): w_block = lax.all_gather(w_factor, 'gram', axis=0, tiled=True)  10.9 us
    ppermute x6, waiting for transfers between devices, send_h(): return lax.ppermute(x, 'doc', partner(OUTER, inner_h, by_outer, by_inner))  8.6 us
    pallas_call x2, Pallas kernels, run_kernel(): pl.pallas_call(functools.partial(kernel, group, side, inner), out_shape=o...  4.04 us
    ppermute x4, starting transfers between devices, send_w(): return lax.ppermute(x, 'gram', partner(OUTER, inner_w, by_outer, by_inner))  3.56 us
  transfers between devices with their start and end apart: 10, of which 4 were waited for; matrix products, arithmetic and copies ran while one was open for 3% of the time, Pallas kernels for 9%

profile of v1, /device:TPU:0, one launch (start us, length us, event | category | flops | bytes accessed | tf_op | source)
XLA Modules:
  0.0 43.1 jit_solution(807447591208688265)
XLA Ops:
  0.6 5.1 %collective-permute-start = (bf16[384,256]{1,0:T(8,128)(2,1)}, bf16[384,256]{1,0:T(8,128)(2,1)S(1)}, u32[]{:S(2)}, u32[]{:S(2)}) collective-permute-start(bf16[384,256]{1,0:T(8,128)(2,1)} %refs_0_.1), channel_id=1, source_target_pairs={{0,24},{8,16},{16,8},{24,0},{1,25},{9,17},{17,9},{25,1},{2,26},{10... | collective-permute-start | bytes 589832 | tf_op jit(solution)/shard_map/ppermute | solution.py:215
  5.7 0.0 collective-permute-start.3
  5.7 0.6 %collective-permute-start.2 = (bf16[384,256]{1,0:T(8,128)(2,1)}, bf16[384,256]{1,0:T(8,128)(2,1)S(1)}, u32[]{:S(2)}, u32[]{:S(2)}) collective-permute-start(bf16[384,256]{1,0:T(8,128)(2,1)} %refs_0_.1), channel_id=1, source_target_pairs={{0,8},{8,0},{16,24},{24,16},{1,9},{9,1},{17,25},{25,17},{2,10},{10... | collective-permute-start | bytes 589832 | tf_op jit(solution)/shard_map/ppermute | solution.py:215
  7.0 10.9 %all_gather.3.w_block = bf16[1536,256]{1,0:T(8,128)(2,1)S(1)} all-gather(bf16[192,256]{1,0:T(8,128)(2,1)} %param.6), channel_id=1, replica_groups=mesh['doc'=4,'gram'=8] {'gram'}, dimensions={0}, use_global_device_ids=true | all-gather | bytes 884736 | tf_op jit(solution)/shard_map/all_gather | solution.py:229
  17.9 0.0 collective-permute-done.refs_0_
  17.9 1.4 %shard_map.77 = (f32[1544,256]{1,0:T(8,128)S(1)}, bf16[24,128,128]{2,1,0:T(8,128)(2,1)S(1)}, f32[392,256]{1,0:T(8,128)S(1)}) custom-call(s32[1,1,24]{2,1,0:T(1,128)} %rows_in.3, s32[1,1,24]{2,1,0:T(1,128)} %cols_in.3, s32[1,1]{1,0:T(1,128)S(6)} %copy.8.live, bf16[1,1,24,128,128]{4,3,2,1,0:T(8,128)(2,1)} %stored.1, bf16[1536,256]{1,0:T(8,128)(2,1)S(1)} %all_gather.3.w_block, ...), custom_call_target="tpu_custom_call" | custom-call | flops 150994944 | bytes 8388608 | tf_op jit(solution)/shard_map/pallas_call | solution.py:194
  19.4 3.0 %collective-permute-start.1 = (f16[392,256]{1,0:T(8,128)(2,1)S(1)}, f16[392,256]{1,0:T(8,128)(2,1)S(1)}, u32[]{:S(2)}, u32[]{:S(2)}) collective-permute-start(f16[392,256]{1,0:T(8,128)(2,1)S(1)} %multiply_convert_fusion.1), channel_id=1, source_target_pairs={{0,8},{8,0},{16,24},{24,16},{1,9},{9,1},{17,25},{25,17},{2,10},{10... | collective-permute-start | bytes 602120 | tf_op jit(solution)/shard_map/ppermute | solution.py:215
  22.5 0.2 collective-permute-done.3.refs_2_
  22.6 0.0 collective-permute-done.2.refs_1_
  22.6 2.6 %shard_map.78 = (f32[4,200,256]{2,1,0:T(8,128)S(1)}, f32[4,200,256]{2,1,0:T(8,128)S(1)}, f32[392,256]{1,0:T(8,128)S(1)}, f32[392,256]{1,0:T(8,128)S(1)}, f32[392,256]{1,0:T(8,128)S(1)}) custom-call(s32[1,1,24]{2,1,0:T(1,128)} %rows_in.3, s32[1,1,24]{2,1,0:T(1,128)} %cols_in.3, s32[1,1]{1,0:T(1,128)S(6)} %copy.8.live, ...), custom_call_target="tpu_custom_call" | custom-call | flops 452984832 | bytes 8388608 | tf_op jit(solution)/shard_map/pallas_call | solution.py:194
  25.3 2.4 %collective-permute-done.1 = f16[392,256]{1,0:T(8,128)(2,1)S(1)} collective-permute-done((f16[392,256]{1,0:T(8,128)(2,1)S(1)}, f16[392,256]{1,0:T(8,128)(2,1)S(1)}, u32[]{:S(2)}, u32[]{:S(2)}) %collective-permute-start.1) | collective-permute-done | bytes 200736 | tf_op jit(solution)/shard_map/ppermute | solution.py:215
  27.7 0.0 collective-permute-start.4
  27.7 0.1 add_convert_fusion
  27.8 2.8 %collective-permute-start.5 = (f16[392,256]{1,0:T(8,128)(2,1)S(1)}, f16[392,256]{1,0:T(8,128)(2,1)S(1)}, u32[]{:S(2)}, u32[]{:S(2)}) collective-permute-start(f16[392,256]{1,0:T(8,128)(2,1)S(1)} %add_convert_fusion), channel_id=1, source_target_pairs={{0,16},{8,24},{16,0},{24,8},{1,17},{9,25},{17,1},{25,9},{2,18},{10... | collective-permute-start | bytes 602120 | tf_op jit(solution)/shard_map/ppermute | solution.py:215
  30.7 0.0 collective-permute-done.4
  30.7 1.1 %collective-permute-start.6 = (f16[392,256]{1,0:T(8,128)(2,1)S(1)}, f16[392,256]{1,0:T(8,128)(2,1)S(1)}, u32[]{:S(2)}, u32[]{:S(2)}) collective-permute-start(f16[392,256]{1,0:T(8,128)(2,1)S(1)} %multiply_convert_fusion), channel_id=1, source_target_pairs={{0,8},{8,0},{16,24},{24,16},{1,9},{9,1},{17,25},{25,17},{2,10},{10... | collective-permute-start | bytes 602120 | tf_op jit(solution)/shard_map/ppermute | solution.py:215
  31.7 0.1 add.21
  31.8 0.0 copy-start
  31.9 0.1 fusion.13
  31.9 0.0 copy-start.1
  31.9 1.5 %collective-permute-start.9 = (f16[200,256]{1,0:T(8,128)(2,1)S(1)}, f16[200,256]{1,0:T(8,128)(2,1)S(1)}, u32[]{:S(2)}, u32[]{:S(2)}) collective-permute-start(f16[200,256]{1,0:T(8,128)(2,1)S(1)} %get-tuple-element.36), channel_id=1, source_target_pairs={{0,6},{1,7},{2,4},{3,5},{4,2},{5,3},{6,0},{7,1},{8,14},{9,15},{10,... | collective-permute-start | bytes 307208 | tf_op jit(solution)/shard_map/ppermute | solution.py:218
  33.5 1.1 %collective-permute-start.8 = (f16[200,256]{1,0:T(8,128)(2,1)S(1)}, f16[200,256]{1,0:T(8,128)(2,1)S(1)}, u32[]{:S(2)}, u32[]{:S(2)}) collective-permute-start(f16[200,256]{1,0:T(8,128)(2,1)S(1)} %get-tuple-element.37), channel_id=1, source_target_pairs={{0,4},{1,5},{2,6},{3,7},{4,0},{5,1},{6,2},{7,3},{8,12},{9,13},{10,... | collective-permute-start | bytes 307208 | tf_op jit(solution)/shard_map/ppermute | solution.py:218
  34.6 0.9 %collective-permute-start.7 = (f16[200,256]{1,0:T(8,128)(2,1)S(1)}, f16[200,256]{1,0:T(8,128)(2,1)S(1)}, u32[]{:S(2)}, u32[]{:S(2)}) collective-permute-start(f16[200,256]{1,0:T(8,128)(2,1)S(1)} %get-tuple-element.38), channel_id=1, source_target_pairs={{0,2},{1,3},{2,0},{3,1},{4,6},{5,7},{6,4},{7,5},{8,10},{9,11},{10,... | collective-permute-start | bytes 307208 | tf_op jit(solution)/shard_map/ppermute | solution.py:218
  35.5 5.2 %collective-permute-done.5 = f16[392,256]{1,0:T(8,128)(2,1)S(1)} collective-permute-done((f16[392,256]{1,0:T(8,128)(2,1)S(1)}, f16[392,256]{1,0:T(8,128)(2,1)S(1)}, u32[]{:S(2)}, u32[]{:S(2)}) %collective-permute-start.5) | collective-permute-done | bytes 200736 | tf_op jit(solution)/shard_map/ppermute | solution.py:215
  40.7 0.7 %collective-permute-done.6 = f16[392,256]{1,0:T(8,128)(2,1)S(1)} collective-permute-done((f16[392,256]{1,0:T(8,128)(2,1)S(1)}, f16[392,256]{1,0:T(8,128)(2,1)S(1)}, u32[]{:S(2)}, u32[]{:S(2)}) %collective-permute-start.6) | collective-permute-done | bytes 200736 | tf_op jit(solution)/shard_map/ppermute | solution.py:215
  41.5 0.1 convert_add_fusion
  41.6 0.0 copy-done
  41.6 0.7 %fusion.1 = bf16[384,256]{1,0:T(8,128)(2,1)} fusion(f32[392,256]{1,0:T(8,128)S(1)} %convert_add_fusion, bf16[384,256]{1,0:T(8,128)(2,1)S(1)} %copy-done, f32[256]{0:T(256)S(1)} %slice_reduce_fusion.1), kind=kLoop, calls=%fused_computation.6 | loop fusion | flops 393216 | bytes 787456 | tf_op jit(solution)/shard_map/convert_element_type | solution.py:287
  42.4 0.0 collective-permute-done.9
  42.4 0.0 collective-permute-done.8
  42.4 0.0 collective-permute-done.7
  42.4 0.1 fusion.8
  42.5 0.0 copy-done.1
  42.5 0.7 %fusion.10 = bf16[192,256]{1,0:T(8,128)(2,1)} fusion(f32[200,256]{1,0:T(8,128)S(1)} %fusion.8, bf16[192,256]{1,0:T(8,128)(2,1)S(1)} %copy-done.1, f32[256]{0:T(256)S(1)} %slice_reduce_fusion), kind=kLoop, calls=%fused_computation.20 | loop fusion | flops 196608 | bytes 394240 | tf_op jit(solution)/shard_map/convert_element_type | solution.py:294
  (4 shorter events, 0.1 us)
Async XLA Ops:
  0.6 17.3 %collective-permute-start = (bf16[384,256]{1,0:T(8,128)(2,1)}, bf16[384,256]{1,0:T(8,128)(2,1)S(1)}, u32[]{:S(2)}, u32[]{:S(2)}) collective-permute-start(bf16[384,256]{1,0:T(8,128)(2,1)} %refs_0_.1), channel_id=1, source_target_pairs={{0,24},{8,16},{16,8},{24,0},{1,25},{9,17},{17,9},{25,1},{2,26},{10... | collective-permute-start | bytes 589832 | tf_op jit(solution)/shard_map/ppermute | solution.py:215
  5.7 16.9 %collective-permute-start.3 = (bf16[384,256]{1,0:T(8,128)(2,1)}, bf16[384,256]{1,0:T(8,128)(2,1)S(1)}, u32[]{:S(2)}, u32[]{:S(2)}) collective-permute-start(bf16[384,256]{1,0:T(8,128)(2,1)} %refs_0_.1), channel_id=1, source_target_pairs={{0,16},{8,24},{16,0},{24,8},{1,17},{9,25},{17,1},{25,9},{2,18},{10... | collective-permute-start | bytes 589832 | tf_op jit(solution)/shard_map/ppermute | solution.py:215
  5.7 16.9 %collective-permute-start.2 = (bf16[384,256]{1,0:T(8,128)(2,1)}, bf16[384,256]{1,0:T(8,128)(2,1)S(1)}, u32[]{:S(2)}, u32[]{:S(2)}) collective-permute-start(bf16[384,256]{1,0:T(8,128)(2,1)} %refs_0_.1), channel_id=1, source_target_pairs={{0,8},{8,0},{16,24},{24,16},{1,9},{9,1},{17,25},{25,17},{2,10},{10... | collective-permute-start | bytes 589832 | tf_op jit(solution)/shard_map/ppermute | solution.py:215
  19.4 8.3 %collective-permute-start.1 = (f16[392,256]{1,0:T(8,128)(2,1)S(1)}, f16[392,256]{1,0:T(8,128)(2,1)S(1)}, u32[]{:S(2)}, u32[]{:S(2)}) collective-permute-start(f16[392,256]{1,0:T(8,128)(2,1)S(1)} %multiply_convert_fusion.1), channel_id=1, source_target_pairs={{0,8},{8,0},{16,24},{24,16},{1,9},{9,1},{17,25},{25,17},{2,10},{10... | collective-permute-start | bytes 602120 | tf_op jit(solution)/shard_map/ppermute | solution.py:215
  27.7 3.0 %collective-permute-start.4 = (f32[4,200,256]{2,1,0:T(8,128)S(1)}, f32[4,200,256]{2,1,0:T(8,128)S(1)}, u32[]{:S(2)}, u32[]{:S(2)}) collective-permute-start(f32[4,200,256]{2,1,0:T(8,128)S(1)} %get-tuple-element.26), channel_id=1, source_target_pairs={{0,1},{1,0},{2,3},{3,2},{4,5},{5,4},{6,7},{7,6},{8,9},{9,8},{10,11... | collective-permute-start | bytes 2457608 | tf_op jit(solution)/shard_map/ppermute | solution.py:218
  27.8 12.9 %collective-permute-start.5 = (f16[392,256]{1,0:T(8,128)(2,1)S(1)}, f16[392,256]{1,0:T(8,128)(2,1)S(1)}, u32[]{:S(2)}, u32[]{:S(2)}) collective-permute-start(f16[392,256]{1,0:T(8,128)(2,1)S(1)} %add_convert_fusion), channel_id=1, source_target_pairs={{0,16},{8,24},{16,0},{24,8},{1,17},{9,25},{17,1},{25,9},{2,18},{10... | collective-permute-start | bytes 602120 | tf_op jit(solution)/shard_map/ppermute | solution.py:215
  30.7 10.8 %collective-permute-start.6 = (f16[392,256]{1,0:T(8,128)(2,1)S(1)}, f16[392,256]{1,0:T(8,128)(2,1)S(1)}, u32[]{:S(2)}, u32[]{:S(2)}) collective-permute-start(f16[392,256]{1,0:T(8,128)(2,1)S(1)} %multiply_convert_fusion), channel_id=1, source_target_pairs={{0,8},{8,0},{16,24},{24,16},{1,9},{9,1},{17,25},{25,17},{2,10},{10... | collective-permute-start | bytes 602120 | tf_op jit(solution)/shard_map/ppermute | solution.py:215
  31.8 9.8 %copy-start = (bf16[384,256]{1,0:T(8,128)(2,1)S(1)}, bf16[384,256]{1,0:T(8,128)(2,1)}, u32[]{:S(2)}) copy-start(bf16[384,256]{1,0:T(8,128)(2,1)} %refs_0_.1) | copy-start | bytes 589828
  31.9 10.5 %copy-start.1 = (bf16[192,256]{1,0:T(8,128)(2,1)S(1)}, bf16[192,256]{1,0:T(8,128)(2,1)}, u32[]{:S(2)}) copy-start(bf16[192,256]{1,0:T(8,128)(2,1)} %param.6) | copy-start | bytes 294916
  31.9 10.4 %collective-permute-start.9 = (f16[200,256]{1,0:T(8,128)(2,1)S(1)}, f16[200,256]{1,0:T(8,128)(2,1)S(1)}, u32[]{:S(2)}, u32[]{:S(2)}) collective-permute-start(f16[200,256]{1,0:T(8,128)(2,1)S(1)} %get-tuple-element.36), channel_id=1, source_target_pairs={{0,6},{1,7},{2,4},{3,5},{4,2},{5,3},{6,0},{7,1},{8,14},{9,15},{10,... | collective-permute-start | bytes 307208 | tf_op jit(solution)/shard_map/ppermute | solution.py:218
  33.5 8.9 %collective-permute-start.8 = (f16[200,256]{1,0:T(8,128)(2,1)S(1)}, f16[200,256]{1,0:T(8,128)(2,1)S(1)}, u32[]{:S(2)}, u32[]{:S(2)}) collective-permute-start(f16[200,256]{1,0:T(8,128)(2,1)S(1)} %get-tuple-element.37), channel_id=1, source_target_pairs={{0,4},{1,5},{2,6},{3,7},{4,0},{5,1},{6,2},{7,3},{8,12},{9,13},{10,... | collective-permute-start | bytes 307208 | tf_op jit(solution)/shard_map/ppermute | solution.py:218
  34.6 7.8 %collective-permute-start.7 = (f16[200,256]{1,0:T(8,128)(2,1)S(1)}, f16[200,256]{1,0:T(8,128)(2,1)S(1)}, u32[]{:S(2)}, u32[]{:S(2)}) collective-permute-start(f16[200,256]{1,0:T(8,128)(2,1)S(1)} %get-tuple-element.38), channel_id=1, source_target_pairs={{0,2},{1,3},{2,0},{3,1},{4,6},{5,7},{6,4},{7,5},{8,10},{9,11},{10,... | collective-permute-start | bytes 307208 | tf_op jit(solution)/shard_map/ppermute | solution.py:218

commit v2 on v1

--- a/solution.py
+++ b/solution.py
@@ -13,7 +13,8 @@
 STEP_SUM = 4
 SCALE = 2.0**-5
 FIRST_GROUP = (3,)
-LAST_GROUP = (0, 1, 2)
+MIDDLE_GROUP = (0, 1)
+LAST_GROUP = (2,)
 
 
 def partner(outer, inner, by_outer, by_inner):
@@ -29,9 +30,7 @@
     return jnp.sum(block.astype(jnp.float32).reshape(rows // EXTRA, EXTRA, k), axis=0)
 
 
-def visit_tiles(
-    group, side, w_ref, counts, acc, h_outs, order, ratios, h_all, h_sum, rows, cols, live
-):
+def visit_tiles(group, side, w_ref, counts, ready, acc, h_out, order, ratios, h_all, rows, cols, live):
     quarter = h_all.shape[0] // len(group)
     me_h = lax.axis_index("doc") // (lax.axis_size("doc") // OUTER)
 
@@ -57,14 +56,14 @@
         for k, member in enumerate(group):
             at = jnp.where(near == member, k, at)
         row = pl.multiple_of(rows[0, 0, slot] * side, side)
-        col = at * quarter + lax.rem(cols[0, 0, slot] * side, quarter)
-        return slot, row, pl.multiple_of(col, side)
+        local = pl.multiple_of(lax.rem(cols[0, 0, slot] * side, quarter), side)
+        return slot, row, at, local, pl.multiple_of(at * quarter + local, side)
 
     def make_ratios(step, carry):
         made = []
         for k in range(STEP_RATIO):
             j = step * STEP_RATIO + k
-            slot, row, col = tile_at(j)
+            slot, row, _, _, col = tile_at(j)
             model = lax.dot_general(
                 w_ref[pl.ds(row, side), :],
                 h_all[pl.ds(col, side), :],
@@ -81,7 +80,7 @@
         terms = []
         for k in range(STEP_SUM):
             j = step * STEP_SUM + k
-            slot, row, col = tile_at(j)
+            slot, row, at, local, col = tile_at(j)
             ratio = ratios[j]
             w_part = jnp.dot(
                 ratio, h_all[pl.ds(col, side), :], preferred_element_type=jnp.float32
@@ -92,24 +91,27 @@
                 (((0,), (0,)), ((), ())),
                 preferred_element_type=jnp.float32,
             )
-            terms.append((row, col, w_part, h_part))
-        for row, col, w_part, h_part in terms:
+            terms.append((row, at, local, w_part, h_part))
+        for row, at, local, w_part, h_part in terms:
             acc[pl.ds(row, side), :] += w_part
-            h_sum[pl.ds(col, side), :] += h_part
+            h_out[at, pl.ds(local, side), :] += h_part
         return carry
 
+    if ready is not None:
+        ready()
     lax.fori_loop(0, (found + STEP_RATIO - 1) // STEP_RATIO, make_ratios, 0)
     lax.fori_loop(0, (found + STEP_SUM - 1) // STEP_SUM, add_terms, 0)
 
-    w_sums = partial_sums(w_ref[...])
-    for at, h_out in enumerate(h_outs):
-        h_out[:quarter, :] = h_sum[at * quarter : (at + 1) * quarter, :]
-        h_out[quarter:, :] = w_sums
-
-
-def started(sems, *pairs):
+
+def clear(h_out, quarter, w_sums):
+    for at in range(h_out.shape[0]):
+        h_out[at, :quarter, :] = jnp.zeros((quarter, h_out.shape[2]), jnp.float32)
+        h_out[at, quarter:, :] = w_sums
+
+
+def started(sems, first, *pairs):
     copies = [
-        pltpu.make_async_copy(source, target, sems.at[k])
+        pltpu.make_async_copy(source, target, sems.at[first + k])
         for k, (source, target) in enumerate(pairs)
     ]
     for copy in copies:
@@ -117,46 +119,66 @@
     return copies
 
 
-def first_kernel(group, side, inner, rows_in, cols_in, live, stored, w_block, *refs):
+def first_kernel(group, side, inner, rows_in, cols_in, live, stored, w_pieces, *refs):
     h_pieces, refs = refs[: len(group)], refs[len(group) :]
-    acc, counts, refs = refs[0], refs[1], refs[2:]
-    h_outs, refs = refs[: len(group)], refs[len(group) :]
-    sems, order, ratios, h_all, h_sum, rows, cols = refs
-    copies = started(sems, (rows_in, rows), (cols_in, cols), (stored.at[0, 0], counts))
+    w_block, acc, counts, w_sums, h_out, sems, order, ratios, h_all, rows, cols = refs
+    places = started(sems, 0, (rows_in, rows), (cols_in, cols))
+    (load,) = started(sems, 2, (stored.at[0, 0], counts))
     quarter = h_pieces[0].shape[0]
     w_len = w_block.shape[0]
+    w_rows = w_len // (inner * OUTER)
+    me_o = lax.axis_index("gram") // inner
+    for o in range(OUTER):
+        for i in range(inner):
+            at = pl.multiple_of(((me_o ^ o) * inner + i) * w_rows, 16)
+            w_block[pl.ds(at, w_rows), :] = w_pieces[i, o]
     for at, piece in enumerate(h_pieces):
         h_all[at * quarter : (at + 1) * quarter, :] = piece[...]
     acc[:w_len, :] = jnp.zeros((w_len, acc.shape[1]), jnp.float32)
     acc[w_len:, :] = partial_sums(h_all[...])
-    h_sum[...] = jnp.zeros_like(h_sum)
-    for copy in copies:
+    w_sums[...] = partial_sums(w_block[...])
+    clear(h_out, quarter, w_sums[...])
+    for copy in places:
         copy.wait()
     visit_tiles(
-        group, side, w_block, counts, acc, h_outs, order, ratios, h_all, h_sum, rows, cols, live
-    )
-
-
-def last_kernel(group, side, inner, rows_in, cols_in, live, counts, w_block, acc_in, *refs):
+        group, side, w_block, counts, load.wait, acc, h_out, order, ratios, h_all, rows, cols, live
+    )
+
+
+def middle_kernel(group, side, inner, rows_in, cols_in, live, counts, w_block, _, w_sums, *refs):
     mine, h_pieces, refs = refs[0], refs[1 : len(group)], refs[len(group) :]
-    w_outs, refs = refs[:inner], refs[inner:]
-    h_outs, refs = refs[: len(group)], refs[len(group) :]
-    sems, order, ratios, h_all, h_sum, rows, cols, acc = refs
+    acc, h_out, sems, order, ratios, h_all, rows, cols = refs
     quarter = mine.shape[0]
-    copies = started(
-        sems, (rows_in, rows), (cols_in, cols), (mine, h_all.at[pl.ds(0, quarter)])
-    )
+    places = started(sems, 0, (rows_in, rows), (cols_in, cols))
+    (load,) = started(sems, 2, (mine, h_all.at[pl.ds(0, quarter)]))
+    w_len = w_block.shape[0]
+    for at, piece in enumerate(h_pieces):
+        h_all[(at + 1) * quarter : (at + 2) * quarter, :] = piece[...]
+    clear(h_out, quarter, w_sums[...])
+    for copy in places:
+        copy.wait()
+    visit_tiles(
+        group, side, w_block, counts, load.wait, acc, h_out, order, ratios, h_all, rows, cols, live
+    )
+    acc[w_len:, :] += partial_sums(h_all[...])
+
+
+def last_kernel(group, side, inner, rows_in, cols_in, live, counts, w_block, _, w_sums, *refs):
+    h_pieces, refs = refs[: len(group)], refs[len(group) :]
+    acc, h_out, w_outs, refs = refs[0], refs[1], refs[2 : 2 + inner], refs[2 + inner :]
+    sems, order, ratios, h_all, rows, cols = refs
+    quarter = h_pieces[0].shape[0]
+    places = started(sems, 0, (rows_in, rows), (cols_in, cols))
     w_len = w_block.shape[0]
     w_rows = w_len // (inner * OUTER)
     for at, piece in enumerate(h_pieces):
-        h_all[(at + 1) * quarter : (at + 2) * quarter, :] = piece[...]
-    acc[:w_len, :] = acc_in[:w_len, :]
-    h_sum[...] = jnp.zeros_like(h_sum)
-    for copy in copies:
+        h_all[at * quarter : (at + 1) * quarter, :] = piece[...]
+    acc[w_len:, :] += partial_sums(h_all[...])
+    clear(h_out, quarter, w_sums[...])
+    for copy in places:
         copy.wait()
-    acc[w_len:, :] = acc_in[w_len:, :] + partial_sums(h_all[...])
     visit_tiles(
-        group, side, w_block, counts, acc, h_outs, order, ratios, h_all, h_sum, rows, cols, live
+        group, side, w_block, counts, None, acc, h_out, order, ratios, h_all, rows, cols, live
     )
     me_w = lax.axis_index("gram")
     me_o, me_i = me_w // inner, lax.rem(me_w, inner)
@@ -165,6 +187,24 @@
             at = pl.multiple_of(((me_o ^ o) * inner + (me_i ^ i)) * w_rows, 8)
             w_outs[i][o, :w_rows, :] = acc[pl.ds(at, w_rows), :]
             w_outs[i][o, w_rows:, :] = acc[w_len:, :]
+
+
+def finish_kernel(w_factor, h_factor, w_total, h_total, w_next, h_next):
+    for factor, total, out in ((h_factor, h_total, h_next), (w_factor, w_total, w_next)):
+        rows = factor.shape[0]
+        denom = jnp.sum(total[rows:, :], axis=0, keepdims=True)
+        out[...] = (factor[...].astype(jnp.float32) * total[:rows, :] / denom).astype(out.dtype)
+
+
+def finish(w_factor, h_factor, w_total, h_total):
+    vmem = pl.BlockSpec(memory_space=pltpu.VMEM)
+    return pl.pallas_call(
+        finish_kernel,
+        out_shape=[jax.ShapeDtypeStruct(x.shape, x.dtype) for x in (w_factor, h_factor)],
+        in_specs=[vmem] * 4,
+        out_specs=[vmem] * 2,
+        compiler_params=pltpu.CompilerParams(vmem_limit_bytes=16 * 1024 * 1024),
+    )(w_factor, h_factor, w_total, h_total)
 
 
 def in_hbm(x):
@@ -182,12 +222,9 @@
         pltpu.SMEM((slots + pad,), jnp.int32),
         pltpu.VMEM((slots + pad, side, side), jnp.bfloat16),
         pltpu.VMEM((width * quarter, topics), jnp.bfloat16),
-        pltpu.VMEM((width * quarter, topics), jnp.float32),
         pltpu.SMEM(rows.shape, rows.dtype),
         pltpu.SMEM(cols.shape, cols.dtype),
     ]
-    if kernel is last_kernel:
-        scratch.append(pltpu.VMEM(acc_shape, jnp.float32))
     spaces = [pltpu.HBM if at in from_hbm else pltpu.VMEM for at in range(len(args))]
     spaces[2] = pltpu.SMEM
     args = [in_hbm(x) if at in from_hbm else x for at, x in enumerate(args)]
@@ -197,6 +234,7 @@
         in_specs=[pl.BlockSpec(memory_space=space) for space in spaces],
         out_specs=[pl.BlockSpec(memory_space=pltpu.VMEM)] * len(out_shapes),
         scratch_shapes=scratch,
+        input_output_aliases={} if kernel is first_kernel else {5: 0},
         compiler_params=pltpu.CompilerParams(vmem_limit_bytes=32 * 1024 * 1024),
         cost_estimate=pl.CostEstimate(
             flops=36 * width * side * side * topics, bytes_accessed=1 << 23, transcendentals=0
@@ -224,38 +262,63 @@
         mine = h_factor
     quarter = mine.shape[0]
     h_pieces = {0: mine}
-    for m in (3, 2, 1):
-        h_pieces[m] = send_h(mine, m)
-    w_block = lax.all_gather(w_factor, "gram", axis=0, tiled=True)
+    h_pieces[3] = send_h(mine, 3)
+    w_got = [send_w(w_factor, o) for o in range(1, OUTER)]
+    h_pieces[2] = send_h(h_pieces[3], 1)
+    later, w_got[0] = lax.optimization_barrier((mine, w_got[0]))
+    h_pieces[1] = send_h(later, 1)
+    w_outer = jnp.stack([w_factor] + w_got)
+    pairs = [[o * inner_w + i for i in range(inner_w)] for o in range(OUTER)]
+    w_pieces = lax.all_gather(w_outer, "gram", axis_index_groups=pairs)
 
     places = [tile_rows, tile_cols, tile_live]
     acc_shape = jax.ShapeDtypeStruct((w_len + EXTRA, topics), jnp.float32)
-    h_shape = jax.ShapeDtypeStruct((quarter + EXTRA, topics), jnp.float32)
+    h_shape = [
+        jax.ShapeDtypeStruct((len(group), quarter + EXTRA, topics), jnp.float32)
+        for group in (FIRST_GROUP, MIDDLE_GROUP, LAST_GROUP)
+    ]
+    sum_shape = jax.ShapeDtypeStruct((EXTRA, topics), jnp.float32)
     w_shape = jax.ShapeDtypeStruct((OUTER, w_rows + EXTRA, topics), jnp.float32)
-    acc, counts, far = run_kernel(
+    w_block, acc, counts, w_sums, far = run_kernel(
         first_kernel,
         FIRST_GROUP,
         inner_w,
-        [*places, tile_counts, w_block, *[h_pieces[m] for m in FIRST_GROUP]],
+        [*places, tile_counts, w_pieces, *[h_pieces[m] for m in FIRST_GROUP]],
         (0, 1, 3),
-        [acc_shape, jax.ShapeDtypeStruct(tile_counts.shape[2:], tile_counts.dtype), h_shape],
+        [
+            jax.ShapeDtypeStruct((w_len, topics), w_factor.dtype),
+            acc_shape,
+            jax.ShapeDtypeStruct(tile_counts.shape[2:], tile_counts.dtype),
+            sum_shape,
+            h_shape[0],
+        ],
         quarter,
         acc_shape.shape,
     )
     h_scale = SCALE / 2
-    far = send_h((far * h_scale).astype(jnp.float16), 1)
-    outs = run_kernel(
+    far = send_h((far[0] * h_scale).astype(jnp.float16), 1)
+    acc, middle = run_kernel(
+        middle_kernel,
+        MIDDLE_GROUP,
+        inner_w,
+        [*places, counts, w_block, acc, w_sums, *[h_pieces[m] for m in MIDDLE_GROUP]],
+        (0, 1, 7),
+        [acc_shape, h_shape[1]],
+        quarter,
+        acc_shape.shape,
+    )
+    _, last, *w_outs = run_kernel(
         last_kernel,
         LAST_GROUP,
         inner_w,
-        [*places, counts, w_block, acc, *[h_pieces[m] for m in LAST_GROUP]],
-        (0, 1, 6),
-        [w_shape] * inner_w + [h_shape] * len(LAST_GROUP),
+        [*places, counts, w_block, acc, w_sums, *[h_pieces[m] for m in LAST_GROUP]],
+        (0, 1),
+        [acc_shape, h_shape[2]] + [w_shape] * inner_w,
         quarter,
         acc_shape.shape,
     )
-    far, *w_outs = lax.optimization_barrier((far, *outs[:inner_w]))
-    terms = dict(zip(LAST_GROUP, outs[inner_w:]))
+    terms = {0: middle[0], 1: middle[1], 2: last[0]}
+    far, *w_outs = lax.optimization_barrier((far, *w_outs))
     across = (terms[2] * h_scale + far.astype(jnp.float32)).astype(jnp.float16)
     across = send_h(across, 2)
 
@@ -283,15 +346,11 @@
         for i in range(1, inner_h):
             total = total + send_h(share(i), 0, i)
         h_total = total
-    h_denom = jnp.sum(h_total[h_rows:], axis=0)
-    h_next = (h_factor.astype(jnp.float32) * h_total[:h_rows] / h_denom).astype(jnp.bfloat16)
-
-    h_next, *w_sent = lax.optimization_barrier((h_next, *w_sent))
+    h_total, *w_sent = lax.optimization_barrier((h_total, *w_sent))
     w_total = w_terms[0] * w_scale
     for got in w_sent:
         w_total = w_total + got.astype(jnp.float32)
-    w_denom = jnp.sum(w_total[w_rows:], axis=0)
-    w_next = (w_factor.astype(jnp.float32) * w_total[:w_rows] / w_denom).astype(jnp.bfloat16)
+    w_next, h_next = finish(w_factor, h_factor, w_total, h_total)
     return (w_next, h_next)
 
 

time: 42.8 us -> 40.3 us (0.942); the launches traced: 43.1 us -> 40.1 us
  blocking collectives: 10.9 us -> 2.37 us
  Pallas kernels: 4.04 us -> 6.82 us
  starting transfers between devices: 16.3 us -> 18.3 us
  waiting for transfers between devices: 8.61 us -> 9.72 us
  other arithmetic: 1.96 us -> 1.41 us
    all_gather x1, blocking collectives: 10.9 us -> 2.37 us  [body(): w_pieces = lax.all_gather(w_outer, 'gram', axis_index_groups=pairs)]
    ppermute x4 -> x7, starting transfers between devices: 3.56 us -> 8.1 us  [send_w(): return lax.ppermute(x, 'gram', partner(OUTER, inner_w, by_outer, by_inner))]
    ppermute x6, starting transfers between devices: 12.7 us -> 10.2 us  [send_h(): return lax.ppermute(x, 'doc', partner(OUTER, inner_h, by_outer, by_inner))]
    pallas_call x2 -> x3, Pallas kernels: 4.04 us -> 6.05 us  [run_kernel(): pl.pallas_call(functools.partial(kernel, group, side, inner), out_shape=o...]
    convert_element_type x3 -> x1, other arithmetic: 1.45 us -> 0.04 us  [body(): far = send_h((far[0] * h_scale).astype(jnp.float16), 1)]
    ppermute x4 -> x7, waiting for transfers between devices: 0.01 us -> 1.36 us  [send_w(): return lax.ppermute(x, 'gram', partner(OUTER, inner_w, by_outer, by_inner))]
    another operation x0 -> x1, other arithmetic: none -> 0.94 us  [body(): w_outer = jnp.stack([w_factor] + w_got)]
    pallas_call x0 -> x1, Pallas kernels: none -> 0.77 us  [finish(): pl.pallas_call(finish_kernel, out_shape=[jax.ShapeDtypeStruct(x.shape, x....]
  transfers between devices with their start and end apart: 10 -> 13, of which waited for: 4 -> 7; matrix products, arithmetic and copies ran while one was open for 3% -> 3% of each run, Pallas kernels for 9% -> 15%
where the time goes in v2:
time: 40.3 us; the launch traced here: 40.1 us
  starting transfers between devices  18.3 us (45%)
  waiting for transfers between devices  9.72 us (24%)
  Pallas kernels  6.82 us (17%)
  blocking collectives  2.37 us (6%)
  between operations  1.44 us (4%)
  other arithmetic  1.41 us (3%)
    ppermute x6, starting transfers between devices, send_h(): return lax.ppermute(x, 'doc', partner(OUTER, inner_h, by_outer, by_inner))  10.2 us
    ppermute x6, waiting for transfers between devices, send_h(): return lax.ppermute(x, 'doc', partner(OUTER, inner_h, by_outer, by_inner))  8.37 us
    ppermute x7, starting transfers between devices, send_w(): return lax.ppermute(x, 'gram', partner(OUTER, inner_w, by_outer, by_inner))  8.1 us
    pallas_call x3, Pallas kernels, run_kernel(): pl.pallas_call(functools.partial(kernel, group, side, inner), out_shape=o...  6.05 us
    all_gather x1, blocking collectives, body(): w_pieces = lax.all_gather(w_outer, 'gram', axis_index_groups=pairs)  2.37 us
    ppermute x7, waiting for transfers between devices, send_w(): return lax.ppermute(x, 'gram', partner(OUTER, inner_w, by_outer, by_inner))  1.36 us
    another operation x1, other arithmetic, body(): w_outer = jnp.stack([w_factor] + w_got)  0.94 us
  transfers between devices with their start and end apart: 13, of which 7 were waited for; matrix products, arithmetic and copies ran while one was open for 3% of the time, Pallas kernels for 15%

profile of v2, /device:TPU:0, one launch (start us, length us, event | category | flops | bytes accessed | tf_op | source)
XLA Modules:
  0.0 40.1 jit_solution(15232785997492603026)
XLA Ops:
  0.6 3.0 %collective-permute-start = (bf16[192,256]{1,0:T(8,128)(2,1)}, bf16[192,256]{1,0:T(8,128)(2,1)S(1)}, u32[]{:S(2)}, u32[]{:S(2)}) collective-permute-start(bf16[192,256]{1,0:T(8,128)(2,1)} %w_factor.1), channel_id=1, source_target_pairs={{0,2},{1,3},{2,0},{3,1},{4,6},{5,7},{6,4},{7,5},{8,10},{9,11},{10,... | collective-permute-start | bytes 294920 | tf_op jit(solution)/shard_map/ppermute | solution.py:256
  3.6 1.5 %collective-permute-start.2 = (bf16[192,256]{1,0:T(8,128)(2,1)}, bf16[192,256]{1,0:T(8,128)(2,1)S(1)}, u32[]{:S(2)}, u32[]{:S(2)}) collective-permute-start(bf16[192,256]{1,0:T(8,128)(2,1)} %w_factor.1), channel_id=1, source_target_pairs={{0,6},{1,7},{2,4},{3,5},{4,2},{5,3},{6,0},{7,1},{8,14},{9,15},{10,... | collective-permute-start | bytes 294920 | tf_op jit(solution)/shard_map/ppermute | solution.py:256
  5.1 0.1 collective-permute-start.1
  5.2 4.1 %collective-permute-start.3 = (bf16[384,256]{1,0:T(8,128)(2,1)}, bf16[384,256]{1,0:T(8,128)(2,1)S(1)}, u32[]{:S(2)}, u32[]{:S(2)}) collective-permute-start(bf16[384,256]{1,0:T(8,128)(2,1)} %h_factor.1), channel_id=1, source_target_pairs={{0,24},{8,16},{16,8},{24,0},{1,25},{9,17},{17,9},{25,1},{2,26},{10... | collective-permute-start | bytes 589832 | tf_op jit(solution)/shard_map/ppermute | solution.py:253
  9.9 0.0 collective-permute-done
  9.9 0.1 collective-permute-start.5
  10.0 0.2 collective-permute-done.2
  10.1 1.1 %collective-permute-done.1 = bf16[192,256]{1,0:T(8,128)(2,1)S(1)} collective-permute-done((bf16[192,256]{1,0:T(8,128)(2,1)}, bf16[192,256]{1,0:T(8,128)(2,1)S(1)}, u32[]{:S(2)}, u32[]{:S(2)}) %collective-permute-start.1) | collective-permute-done | bytes 98336 | tf_op jit(solution)/shard_map/ppermute | solution.py:256
  11.3 0.9 %pad_maximum_fusion = bf16[4,192,256]{2,1,0:T(8,128)(2,1)S(1)} fusion(bf16[1,192,256]{2,1,0:T(8,128)(2,1)S(1)} %bitcast.34, bf16[1,192,256]{2,1,0:T(8,128)(2,1)S(1)} %bitcast.35, bf16[1,192,256]{2,1,0:T(8,128)(2,1)S(1)} %bitcast.33, bf16[1,192,256]{2,1,0:T(8,128)(2,1)} %bitcast.32), kind=kLoop, calls=%fused_computation.6 | loop fusion | flops 589824 | bytes 786432 | tf_op jit(solution)/shard_map/stack | solution.py:270
  12.2 2.4 %all-gather = bf16[8,192,256]{2,1,0:T(8,128)(2,1)S(1)} all-gather(bf16[4,192,256]{2,1,0:T(8,128)(2,1)S(1)} %pad_maximum_fusion), channel_id=2, replica_groups={{0,1},{2,3},{4,5},{6,7},{8,9},{10,11},{12,13},{14,15},{16,17},{18,19},{..., dimensions={0}, use_global_device_ids=true | all-gather | bytes 1179648 | tf_op jit(solution)/shard_map/all_gather | solution.py:272
  14.6 0.7 %collective-permute-done.3.refs_0_ = bf16[384,256]{1,0:T(8,128)(2,1)S(1)} collective-permute-done((bf16[384,256]{1,0:T(8,128)(2,1)}, bf16[384,256]{1,0:T(8,128)(2,1)S(1)}, u32[]{:S(2)}, u32[]{:S(2)}) %collective-permute-start.3) | collective-permute-done | bytes 196640 | tf_op jit(solution)/shard_map/ppermute | solution.py:253
  15.3 2.2 %collective-permute-start.6 = (bf16[384,256]{1,0:T(8,128)(2,1)S(1)}, bf16[384,256]{1,0:T(8,128)(2,1)S(1)}, u32[]{:S(2)}, u32[]{:S(2)}) collective-permute-start(bf16[384,256]{1,0:T(8,128)(2,1)S(1)} %collective-permute-done.3.refs_0_), channel_id=1, source_target_pairs={{0,8},{8,0},{16,24},{24,16},{1,9},{9,1},{17,25},{25,17},{2,10},{10... | collective-permute-start | bytes 589832 | tf_op jit(solution)/shard_map/ppermute | solution.py:253
  17.5 1.8 %shard_map.77 = (bf16[1536,256]{1,0:T(8,128)(2,1)S(1)}, f32[1544,256]{1,0:T(8,128)S(1)}, bf16[24,128,128]{2,1,0:T(8,128)(2,1)S(1)}, f32[8,256]{1,0:T(8,128)S(1)}, f32[1,392,256]{2,1,0:T(8,128)S(1)}) custom-call(s32[1,1,24]{2,1,0:T(1,128)} %rows_in.5, s32[1,1,24]{2,1,0:T(1,128)} %cols_in.5, s32[1,1]{1,0:T(1,128)S(6)} %copy.12.live, ...), custom_call_target="tpu_custom_call" | custom-call | flops 150994944 | bytes 8388608 | tf_op jit(solution)/shard_map/pallas_call | solution.py:231
  19.3 0.1 collective-permute-start.4
  19.4 0.0 collective-permute-done.5.refs_1_
  19.4 2.1 %shard_map.78 = (f32[1544,256]{1,0:T(8,128)S(1)}, f32[2,392,256]{2,1,0:T(8,128)S(1)}) custom-call(s32[1,1,24]{2,1,0:T(1,128)} %rows_in.5, s32[1,1,24]{2,1,0:T(1,128)} %cols_in.5, s32[1,1]{1,0:T(1,128)S(6)} %copy.12.live, bf16[24,128,128]{2,1,0:T(8,128)(2,1)S(1)} %get-tuple-element.25.counts, ...), custom_call_target="tpu_custom_call", output_to_operand_aliasing={{0}: (5, {})} | custom-call | flops 301989888 | bytes 8388608 | tf_op jit(solution)/shard_map/pallas_call | solution.py:231
  21.6 1.7 %collective-permute-done.6.refs_0_ = bf16[384,256]{1,0:T(8,128)(2,1)S(1)} collective-permute-done((bf16[384,256]{1,0:T(8,128)(2,1)S(1)}, bf16[384,256]{1,0:T(8,128)(2,1)S(1)}, u32[]{:S(2)}, u32[]{:S(2)}) %collective-permute-start.6) | collective-permute-done | bytes 196640 | tf_op jit(solution)/shard_map/ppermute | solution.py:253
  23.2 2.1 %shard_map.79 = (f32[1544,256]{1,0:T(8,128)S(1)}, f32[1,392,256]{2,1,0:T(8,128)S(1)}, f32[4,200,256]{2,1,0:T(8,128)S(1)}, f32[4,200,256]{2,1,0:T(8,128)S(1)}) custom-call(s32[1,1,24]{2,1,0:T(1,128)} %rows_in.5, s32[1,1,24]{2,1,0:T(1,128)} %cols_in.5, s32[1,1]{1,0:T(1,128)S(6)} %copy.12.live, ...), custom_call_target="tpu_custom_call", output_to_operand_aliasing={{0}: (5, {})} | custom-call | flops 150994944 | bytes 8388608 | tf_op jit(solution)/shard_map/pallas_call | solution.py:231
  25.4 1.0 %collective-permute-done.4 = f16[392,256]{1,0:T(8,128)(2,1)S(1)} collective-permute-done((f16[392,256]{1,0:T(8,128)(2,1)S(1)}, f16[392,256]{1,0:T(8,128)(2,1)S(1)}, u32[]{:S(2)}, u32[]{:S(2)}) %collective-permute-start.4) | collective-permute-done | bytes 200736 | tf_op jit(solution)/shard_map/ppermute | solution.py:253
  26.3 0.0 collective-permute-start.7
  26.4 0.1 fusion
  26.5 2.1 %collective-permute-start.8 = (f16[392,256]{1,0:T(8,128)(2,1)S(1)}, f16[392,256]{1,0:T(8,128)(2,1)S(1)}, u32[]{:S(2)}, u32[]{:S(2)}) collective-permute-start(f16[392,256]{1,0:T(8,128)(2,1)S(1)} %fusion), channel_id=1, source_target_pairs={{0,16},{8,24},{16,0},{24,8},{1,17},{9,25},{17,1},{25,9},{2,18},{10... | collective-permute-start | bytes 602120 | tf_op jit(solution)/shard_map/ppermute | solution.py:253
  28.6 0.1 collective-permute-done.7
  28.7 1.7 %collective-permute-start.9 = (f16[392,256]{1,0:T(8,128)(2,1)S(1)}, f16[392,256]{1,0:T(8,128)(2,1)S(1)}, u32[]{:S(2)}, u32[]{:S(2)}) collective-permute-start(f16[392,256]{1,0:T(8,128)(2,1)S(1)} %fusion.10), channel_id=1, source_target_pairs={{0,8},{8,0},{16,24},{24,16},{1,9},{9,1},{17,25},{25,17},{2,10},{10... | collective-permute-start | bytes 602120 | tf_op jit(solution)/shard_map/ppermute | solution.py:253
  30.4 0.1 add.21
  30.5 0.0 copy-start
  30.5 0.0 copy-start.1
  30.5 0.1 fusion.13
  30.6 1.6 %collective-permute-start.10 = (f16[200,256]{1,0:T(8,128)(2,1)S(1)}, f16[200,256]{1,0:T(8,128)(2,1)S(1)}, u32[]{:S(2)}, u32[]{:S(2)}) collective-permute-start(f16[200,256]{1,0:T(8,128)(2,1)S(1)} %get-tuple-element.46), channel_id=1, source_target_pairs={{0,2},{1,3},{2,0},{3,1},{4,6},{5,7},{6,4},{7,5},{8,10},{9,11},{10,... | collective-permute-start | bytes 307208 | tf_op jit(solution)/shard_map/ppermute | solution.py:256
  32.1 1.5 %collective-permute-start.11 = (f16[200,256]{1,0:T(8,128)(2,1)S(1)}, f16[200,256]{1,0:T(8,128)(2,1)S(1)}, u32[]{:S(2)}, u32[]{:S(2)}) collective-permute-start(f16[200,256]{1,0:T(8,128)(2,1)S(1)} %get-tuple-element.45), channel_id=1, source_target_pairs={{0,4},{1,5},{2,6},{3,7},{4,0},{5,1},{6,2},{7,3},{8,12},{9,13},{10,... | collective-permute-start | bytes 307208 | tf_op jit(solution)/shard_map/ppermute | solution.py:256
  33.6 0.5 %collective-permute-start.12 = (f16[200,256]{1,0:T(8,128)(2,1)S(1)}, f16[200,256]{1,0:T(8,128)(2,1)S(1)}, u32[]{:S(2)}, u32[]{:S(2)}) collective-permute-start(f16[200,256]{1,0:T(8,128)(2,1)S(1)} %get-tuple-element.44), channel_id=1, source_target_pairs={{0,6},{1,7},{2,4},{3,5},{4,2},{5,3},{6,0},{7,1},{8,14},{9,15},{10,... | collective-permute-start | bytes 307208 | tf_op jit(solution)/shard_map/ppermute | solution.py:256
  34.1 5.0 %collective-permute-done.8 = f16[392,256]{1,0:T(8,128)(2,1)S(1)} collective-permute-done((f16[392,256]{1,0:T(8,128)(2,1)S(1)}, f16[392,256]{1,0:T(8,128)(2,1)S(1)}, u32[]{:S(2)}, u32[]{:S(2)}) %collective-permute-start.8) | collective-permute-done | bytes 200736 | tf_op jit(solution)/shard_map/ppermute | solution.py:253
  39.1 0.0 collective-permute-done.9
  39.1 0.1 fusion.1.h_total
  39.2 0.0 collective-permute-done.10
  39.2 0.0 collective-permute-done.11
  39.2 0.0 collective-permute-done.12
  39.2 0.1 fusion.8.w_total
  39.3 0.0 copy-done
  39.3 0.0 copy-done.1
  39.3 0.8 %shard_map.80 = (bf16[192,256]{1,0:T(8,128)(2,1)}, bf16[384,256]{1,0:T(8,128)(2,1)}) custom-call(bf16[192,256]{1,0:T(8,128)(2,1)S(1)} %copy-done.1, bf16[384,256]{1,0:T(8,128)(2,1)S(1)} %copy-done, f32[200,256]{1,0:T(8,128)S(1)} %fusion.8.w_total, f32[392,256]{1,0:T(8,128)S(1)} %fusion.1.h_total), custom_call_target="tpu_custom_call" | custom-call | tf_op jit(solution)/shard_map/pallas_call | solution.py:201
  (2 shorter events, 0.1 us)
Async XLA Ops:
  0.6 9.3 %collective-permute-start = (bf16[192,256]{1,0:T(8,128)(2,1)}, bf16[192,256]{1,0:T(8,128)(2,1)S(1)}, u32[]{:S(2)}, u32[]{:S(2)}) collective-permute-start(bf16[192,256]{1,0:T(8,128)(2,1)} %w_factor.1), channel_id=1, source_target_pairs={{0,2},{1,3},{2,0},{3,1},{4,6},{5,7},{6,4},{7,5},{8,10},{9,11},{10,... | collective-permute-start | bytes 294920 | tf_op jit(solution)/shard_map/ppermute | solution.py:256
  3.6 6.5 %collective-permute-start.2 = (bf16[192,256]{1,0:T(8,128)(2,1)}, bf16[192,256]{1,0:T(8,128)(2,1)S(1)}, u32[]{:S(2)}, u32[]{:S(2)}) collective-permute-start(bf16[192,256]{1,0:T(8,128)(2,1)} %w_factor.1), channel_id=1, source_target_pairs={{0,6},{1,7},{2,4},{3,5},{4,2},{5,3},{6,0},{7,1},{8,14},{9,15},{10,... | collective-permute-start | bytes 294920 | tf_op jit(solution)/shard_map/ppermute | solution.py:256
  5.1 6.1 %collective-permute-start.1 = (bf16[192,256]{1,0:T(8,128)(2,1)}, bf16[192,256]{1,0:T(8,128)(2,1)S(1)}, u32[]{:S(2)}, u32[]{:S(2)}) collective-permute-start(bf16[192,256]{1,0:T(8,128)(2,1)} %w_factor.1), channel_id=1, source_target_pairs={{0,4},{1,5},{2,6},{3,7},{4,0},{5,1},{6,2},{7,3},{8,12},{9,13},{10,... | collective-permute-start | bytes 294920 | tf_op jit(solution)/shard_map/ppermute | solution.py:256
  5.2 10.1 %collective-permute-start.3 = (bf16[384,256]{1,0:T(8,128)(2,1)}, bf16[384,256]{1,0:T(8,128)(2,1)S(1)}, u32[]{:S(2)}, u32[]{:S(2)}) collective-permute-start(bf16[384,256]{1,0:T(8,128)(2,1)} %h_factor.1), channel_id=1, source_target_pairs={{0,24},{8,16},{16,8},{24,0},{1,25},{9,17},{17,9},{25,1},{2,26},{10... | collective-permute-start | bytes 589832 | tf_op jit(solution)/shard_map/ppermute | solution.py:253
  9.9 9.5 %collective-permute-start.5 = (bf16[384,256]{1,0:T(8,128)(2,1)}, bf16[384,256]{1,0:T(8,128)(2,1)S(1)}, u32[]{:S(2)}, u32[]{:S(2)}) collective-permute-start(bf16[384,256]{1,0:T(8,128)(2,1)} %h_factor.1), channel_id=1, source_target_pairs={{0,8},{8,0},{16,24},{24,16},{1,9},{9,1},{17,25},{25,17},{2,10},{10... | collective-permute-start | bytes 589832 | tf_op jit(solution)/shard_map/ppermute | solution.py:253
  15.3 8.0 %collective-permute-start.6 = (bf16[384,256]{1,0:T(8,128)(2,1)S(1)}, bf16[384,256]{1,0:T(8,128)(2,1)S(1)}, u32[]{:S(2)}, u32[]{:S(2)}) collective-permute-start(bf16[384,256]{1,0:T(8,128)(2,1)S(1)} %collective-permute-done.3.refs_0_), channel_id=1, source_target_pairs={{0,8},{8,0},{16,24},{24,16},{1,9},{9,1},{17,25},{25,17},{2,10},{10... | collective-permute-start | bytes 589832 | tf_op jit(solution)/shard_map/ppermute | solution.py:253
  19.3 7.0 %collective-permute-start.4 = (f16[392,256]{1,0:T(8,128)(2,1)S(1)}, f16[392,256]{1,0:T(8,128)(2,1)S(1)}, u32[]{:S(2)}, u32[]{:S(2)}) collective-permute-start(f16[392,256]{1,0:T(8,128)(2,1)S(1)} %fusion.9), channel_id=1, source_target_pairs={{0,8},{8,0},{16,24},{24,16},{1,9},{9,1},{17,25},{25,17},{2,10},{10... | collective-permute-start | bytes 602120 | tf_op jit(solution)/shard_map/ppermute | solution.py:253
  26.3 2.3 %collective-permute-start.7 = (f32[4,200,256]{2,1,0:T(8,128)S(1)}, f32[4,200,256]{2,1,0:T(8,128)S(1)}, u32[]{:S(2)}, u32[]{:S(2)}) collective-permute-start(f32[4,200,256]{2,1,0:T(8,128)S(1)} %get-tuple-element.35), channel_id=1, source_target_pairs={{0,1},{1,0},{2,3},{3,2},{4,5},{5,4},{6,7},{7,6},{8,9},{9,8},{10,11... | collective-permute-start | bytes 2457608 | tf_op jit(solution)/shard_map/ppermute | solution.py:256
  26.5 12.7 %collective-permute-start.8 = (f16[392,256]{1,0:T(8,128)(2,1)S(1)}, f16[392,256]{1,0:T(8,128)(2,1)S(1)}, u32[]{:S(2)}, u32[]{:S(2)}) collective-permute-start(f16[392,256]{1,0:T(8,128)(2,1)S(1)} %fusion), channel_id=1, source_target_pairs={{0,16},{8,24},{16,0},{24,8},{1,17},{9,25},{17,1},{25,9},{2,18},{10... | collective-permute-start | bytes 602120 | tf_op jit(solution)/shard_map/ppermute | solution.py:253
  28.7 10.5 %collective-permute-start.9 = (f16[392,256]{1,0:T(8,128)(2,1)S(1)}, f16[392,256]{1,0:T(8,128)(2,1)S(1)}, u32[]{:S(2)}, u32[]{:S(2)}) collective-permute-start(f16[392,256]{1,0:T(8,128)(2,1)S(1)} %fusion.10), channel_id=1, source_target_pairs={{0,8},{8,0},{16,24},{24,16},{1,9},{9,1},{17,25},{25,17},{2,10},{10... | collective-permute-start | bytes 602120 | tf_op jit(solution)/shard_map/ppermute | solution.py:253
  30.5 8.9 %copy-start = (bf16[384,256]{1,0:T(8,128)(2,1)S(1)}, bf16[384,256]{1,0:T(8,128)(2,1)}, u32[]{:S(2)}) copy-start(bf16[384,256]{1,0:T(8,128)(2,1)} %h_factor.1) | copy-start | bytes 589828
  30.5 8.9 %copy-start.1 = (bf16[192,256]{1,0:T(8,128)(2,1)S(1)}, bf16[192,256]{1,0:T(8,128)(2,1)}, u32[]{:S(2)}) copy-start(bf16[192,256]{1,0:T(8,128)(2,1)} %w_factor.1) | copy-start | bytes 294916
  30.6 8.6 %collective-permute-start.10 = (f16[200,256]{1,0:T(8,128)(2,1)S(1)}, f16[200,256]{1,0:T(8,128)(2,1)S(1)}, u32[]{:S(2)}, u32[]{:S(2)}) collective-permute-start(f16[200,256]{1,0:T(8,128)(2,1)S(1)} %get-tuple-element.46), channel_id=1, source_target_pairs={{0,2},{1,3},{2,0},{3,1},{4,6},{5,7},{6,4},{7,5},{8,10},{9,11},{10,... | collective-permute-start | bytes 307208 | tf_op jit(solution)/shard_map/ppermute | solution.py:256
  32.1 7.1 %collective-permute-start.11 = (f16[200,256]{1,0:T(8,128)(2,1)S(1)}, f16[200,256]{1,0:T(8,128)(2,1)S(1)}, u32[]{:S(2)}, u32[]{:S(2)}) collective-permute-start(f16[200,256]{1,0:T(8,128)(2,1)S(1)} %get-tuple-element.45), channel_id=1, source_target_pairs={{0,4},{1,5},{2,6},{3,7},{4,0},{5,1},{6,2},{7,3},{8,12},{9,13},{10,... | collective-permute-start | bytes 307208 | tf_op jit(solution)/shard_map/ppermute | solution.py:256
  33.6 5.6 %collective-permute-start.12 = (f16[200,256]{1,0:T(8,128)(2,1)S(1)}, f16[200,256]{1,0:T(8,128)(2,1)S(1)}, u32[]{:S(2)}, u32[]{:S(2)}) collective-permute-start(f16[200,256]{1,0:T(8,128)(2,1)S(1)} %get-tuple-element.44), channel_id=1, source_target_pairs={{0,6},{1,7},{2,4},{3,5},{4,2},{5,3},{6,0},{7,1},{8,14},{9,15},{10,... | collective-permute-start | bytes 307208 | tf_op jit(solution)/shard_map/ppermute | solution.py:256

commit v3 on v2

--- a/solution.py
+++ b/solution.py
@@ -9,8 +9,8 @@
 
 OUTER = 4
 EXTRA = 8
-STEP_RATIO = 8
-STEP_SUM = 4
+STEP_RATIO = 6
+STEP_SUM = 6
 SCALE = 2.0**-5
 FIRST_GROUP = (3,)
 MIDDLE_GROUP = (0, 1)
@@ -237,7 +237,7 @@
         input_output_aliases={} if kernel is first_kernel else {5: 0},
         compiler_params=pltpu.CompilerParams(vmem_limit_bytes=32 * 1024 * 1024),
         cost_estimate=pl.CostEstimate(
-            flops=36 * width * side * side * topics, bytes_accessed=1 << 23, transcendentals=0
+            flops=144 * width * side * side * topics, bytes_accessed=1 << 23, transcendentals=0
         ),
     )(*args)
 
@@ -262,11 +262,14 @@
         mine = h_factor
     quarter = mine.shape[0]
     h_pieces = {0: mine}
+    w_got = [None] * 3
+    w_got[1] = send_w(w_factor, 2)
+    w_got[0] = send_w(w_factor, 1)
+    w_got[2] = send_w(w_factor, 3)
     h_pieces[3] = send_h(mine, 3)
-    w_got = [send_w(w_factor, o) for o in range(1, OUTER)]
-    h_pieces[2] = send_h(h_pieces[3], 1)
     later, w_got[0] = lax.optimization_barrier((mine, w_got[0]))
     h_pieces[1] = send_h(later, 1)
+    h_pieces[2] = send_h(h_pieces[3], 1)
     w_outer = jnp.stack([w_factor] + w_got)
     pairs = [[o * inner_w + i for i in range(inner_w)] for o in range(OUTER)]
     w_pieces = lax.all_gather(w_outer, "gram", axis_index_groups=pairs)
@@ -318,19 +321,20 @@
         acc_shape.shape,
     )
     terms = {0: middle[0], 1: middle[1], 2: last[0]}
-    far, *w_outs = lax.optimization_barrier((far, *w_outs))
+    far, last, *w_outs = lax.optimization_barrier((far, last, *w_outs))
+    terms[2] = last[0]
     across = (terms[2] * h_scale + far.astype(jnp.float32)).astype(jnp.float16)
     across = send_h(across, 2)
 
     w_scale = SCALE / inner_w
     w_got = [send_w(w_outs[i], 0, i) for i in range(1, inner_w)]
-    near, *w_got = lax.optimization_barrier(((terms[1] * h_scale).astype(jnp.float16), *w_got))
-    near = send_h(near, 1)
     w_terms = w_outs[0]
     for got in w_got:
         w_terms = w_terms + got
+    near, w_terms = lax.optimization_barrier(((terms[1] * h_scale).astype(jnp.float16), w_terms))
+    near = send_h(near, 1)
     w_sent = [
-        send_w((w_terms[o] * w_scale).astype(jnp.float16), o) for o in range(1, OUTER)
+        send_w((w_terms[o] * w_scale).astype(jnp.float16), o) for o in range(OUTER - 1, 0, -1)
     ]
 
     h_total = terms[0] * h_scale + across.astype(jnp.float32) + near.astype(jnp.float32)

time: 40.3 us -> 40.3 us (level)
  waiting for transfers between devices: 9.72 us -> 7.91 us
  Pallas kernels: 6.82 us -> 7.91 us
  starting transfers between devices: 18.3 us -> 19.1 us
    ppermute x6, waiting for transfers between devices: 8.37 us -> 6.95 us  [send_h(): return lax.ppermute(x, 'doc', partner(OUTER, inner_h, by_outer, by_inner))]
    pallas_call x3, Pallas kernels: 6.05 us -> 7.14 us  [run_kernel(): pl.pallas_call(functools.partial(kernel, group, side, inner), out_shape=o...]
    ppermute x6, starting transfers between devices: 10.2 us -> 11 us  [send_h(): return lax.ppermute(x, 'doc', partner(OUTER, inner_h, by_outer, by_inner))]
  transfers between devices with their start and end apart: 13 -> 13, of which waited for: 7 -> 5; matrix products, arithmetic and copies ran while one was open for 3% -> 3% of each run, Pallas kernels for 15% -> 18%
where the time goes in v3:
time: 40.3 us; the launch traced here: 40.1 us
  starting transfers between devices  19.1 us (47%)
  waiting for transfers between devices  7.91 us (20%)
  Pallas kernels  7.91 us (20%)
  blocking collectives  2.37 us (6%)
  other arithmetic  1.43 us (4%)
  between operations  1.42 us (4%)
    ppermute x6, starting transfers between devices, send_h(): return lax.ppermute(x, 'doc', partner(OUTER, inner_h, by_outer, by_inner))  11 us
    ppermute x7, starting transfers between devices, send_w(): return lax.ppermute(x, 'gram', partner(OUTER, inner_w, by_outer, by_inner))  8.1 us
    pallas_call x3, Pallas kernels, run_kernel(): pl.pallas_call(functools.partial(kernel, group, side, inner), out_shape=o...  7.14 us
    ppermute x6, waiting for transfers between devices, send_h(): return lax.ppermute(x, 'doc', partner(OUTER, inner_h, by_outer, by_inner))  6.95 us
    all_gather x1, blocking collectives, body(): w_pieces = lax.all_gather(w_outer, 'gram', axis_index_groups=pairs)  2.37 us
    ppermute x7, waiting for transfers between devices, send_w(): return lax.ppermute(x, 'gram', partner(OUTER, inner_w, by_outer, by_inner))  0.96 us
    another operation x1, other arithmetic, body(): w_outer = jnp.stack([w_factor] + w_got)  0.94 us
  transfers between devices with their start and end apart: 13, of which 5 were waited for; matrix products, arithmetic and copies ran while one was open for 3% of the time, Pallas kernels for 18%

profile of v3, /device:TPU:0, one launch (start us, length us, event | category | flops | bytes accessed | tf_op | source)
XLA Modules:
  0.0 40.1 jit_solution(15913970875814946847)
XLA Ops:
  0.6 3.0 %collective-permute-start = (bf16[192,256]{1,0:T(8,128)(2,1)}, bf16[192,256]{1,0:T(8,128)(2,1)S(1)}, u32[]{:S(2)}, u32[]{:S(2)}) collective-permute-start(bf16[192,256]{1,0:T(8,128)(2,1)} %w_factor.1), channel_id=1, source_target_pairs={{0,2},{1,3},{2,0},{3,1},{4,6},{5,7},{6,4},{7,5},{8,10},{9,11},{10,... | collective-permute-start | bytes 294920 | tf_op jit(solution)/shard_map/ppermute | solution.py:256
  3.6 1.5 %collective-permute-start.1 = (bf16[192,256]{1,0:T(8,128)(2,1)}, bf16[192,256]{1,0:T(8,128)(2,1)S(1)}, u32[]{:S(2)}, u32[]{:S(2)}) collective-permute-start(bf16[192,256]{1,0:T(8,128)(2,1)} %w_factor.1), channel_id=1, source_target_pairs={{0,4},{1,5},{2,6},{3,7},{4,0},{5,1},{6,2},{7,3},{8,12},{9,13},{10,... | collective-permute-start | bytes 294920 | tf_op jit(solution)/shard_map/ppermute | solution.py:256
  5.2 0.0 collective-permute-start.2
  5.2 4.1 %collective-permute-start.3 = (bf16[384,256]{1,0:T(8,128)(2,1)}, bf16[384,256]{1,0:T(8,128)(2,1)S(1)}, u32[]{:S(2)}, u32[]{:S(2)}) collective-permute-start(bf16[384,256]{1,0:T(8,128)(2,1)} %h_factor.1), channel_id=1, source_target_pairs={{0,24},{8,16},{16,8},{24,0},{1,25},{9,17},{17,9},{25,1},{2,26},{10... | collective-permute-start | bytes 589832 | tf_op jit(solution)/shard_map/ppermute | solution.py:253
  9.9 0.0 collective-permute-done
  9.9 0.1 collective-permute-start.4
  10.0 0.0 collective-permute-done.1
  10.0 0.9 %collective-permute-done.2 = bf16[192,256]{1,0:T(8,128)(2,1)S(1)} collective-permute-done((bf16[192,256]{1,0:T(8,128)(2,1)}, bf16[192,256]{1,0:T(8,128)(2,1)S(1)}, u32[]{:S(2)}, u32[]{:S(2)}) %collective-permute-start.2) | collective-permute-done | bytes 98336 | tf_op jit(solution)/shard_map/ppermute | solution.py:256
  10.9 0.9 %pad_maximum_fusion = bf16[4,192,256]{2,1,0:T(8,128)(2,1)S(1)} fusion(bf16[1,192,256]{2,1,0:T(8,128)(2,1)S(1)} %bitcast.33, bf16[1,192,256]{2,1,0:T(8,128)(2,1)S(1)} %bitcast.32, bf16[1,192,256]{2,1,0:T(8,128)(2,1)S(1)} %bitcast.31, bf16[1,192,256]{2,1,0:T(8,128)(2,1)} %bitcast.30), kind=kLoop, calls=%fused_computation.6 | loop fusion | flops 589824 | bytes 786432 | tf_op jit(solution)/shard_map/stack | solution.py:273
  11.8 2.4 %all-gather = bf16[8,192,256]{2,1,0:T(8,128)(2,1)S(1)} all-gather(bf16[4,192,256]{2,1,0:T(8,128)(2,1)S(1)} %pad_maximum_fusion), channel_id=2, replica_groups={{0,1},{2,3},{4,5},{6,7},{8,9},{10,11},{12,13},{14,15},{16,17},{18,19},{..., dimensions={0}, use_global_device_ids=true | all-gather | bytes 1179648 | tf_op jit(solution)/shard_map/all_gather | solution.py:275
  14.2 1.1 %collective-permute-done.3.refs_0_ = bf16[384,256]{1,0:T(8,128)(2,1)S(1)} collective-permute-done((bf16[384,256]{1,0:T(8,128)(2,1)}, bf16[384,256]{1,0:T(8,128)(2,1)S(1)}, u32[]{:S(2)}, u32[]{:S(2)}) %collective-permute-start.3) | collective-permute-done | bytes 196640 | tf_op jit(solution)/shard_map/ppermute | solution.py:253
  15.3 2.2 %collective-permute-start.6 = (bf16[384,256]{1,0:T(8,128)(2,1)S(1)}, bf16[384,256]{1,0:T(8,128)(2,1)S(1)}, u32[]{:S(2)}, u32[]{:S(2)}) collective-permute-start(bf16[384,256]{1,0:T(8,128)(2,1)S(1)} %collective-permute-done.3.refs_0_), channel_id=1, source_target_pairs={{0,8},{8,0},{16,24},{24,16},{1,9},{9,1},{17,25},{25,17},{2,10},{10... | collective-permute-start | bytes 589832 | tf_op jit(solution)/shard_map/ppermute | solution.py:253
  17.4 1.8 %shard_map.77 = (bf16[1536,256]{1,0:T(8,128)(2,1)S(1)}, f32[1544,256]{1,0:T(8,128)S(1)}, bf16[24,128,128]{2,1,0:T(8,128)(2,1)S(1)}, f32[8,256]{1,0:T(8,128)S(1)}, f32[1,392,256]{2,1,0:T(8,128)S(1)}) custom-call(s32[1,1,24]{2,1,0:T(1,128)} %rows_in.5, s32[1,1,24]{2,1,0:T(1,128)} %cols_in.5, s32[1,1]{1,0:T(1,128)S(6)} %copy.12.live, ...), custom_call_target="tpu_custom_call" | custom-call | flops 603979776 | bytes 8388608 | tf_op jit(solution)/shard_map/pallas_call | solution.py:231
  19.3 0.8 %collective-permute-start.5 = (f16[392,256]{1,0:T(8,128)(2,1)S(1)}, f16[392,256]{1,0:T(8,128)(2,1)S(1)}, u32[]{:S(2)}, u32[]{:S(2)}) collective-permute-start(f16[392,256]{1,0:T(8,128)(2,1)S(1)} %fusion.5), channel_id=1, source_target_pairs={{0,8},{8,0},{16,24},{24,16},{1,9},{9,1},{17,25},{25,17},{2,10},{10... | collective-permute-start | bytes 602120 | tf_op jit(solution)/shard_map/ppermute | solution.py:253
  20.1 0.0 collective-permute-done.4.refs_1_
  20.1 2.7 %shard_map.78 = (f32[1544,256]{1,0:T(8,128)S(1)}, f32[2,392,256]{2,1,0:T(8,128)S(1)}) custom-call(s32[1,1,24]{2,1,0:T(1,128)} %rows_in.5, s32[1,1,24]{2,1,0:T(1,128)} %cols_in.5, s32[1,1]{1,0:T(1,128)S(6)} %copy.12.live, bf16[24,128,128]{2,1,0:T(8,128)(2,1)S(1)} %get-tuple-element.25.counts, ...), custom_call_target="tpu_custom_call", output_to_operand_aliasing={{0}: (5, {})} | custom-call | flops 1207959552 | bytes 8388608 | tf_op jit(solution)/shard_map/pallas_call | solution.py:231
  22.8 0.0 collective-permute-done.6.refs_0_
  22.8 2.6 %shard_map.79 = (f32[1544,256]{1,0:T(8,128)S(1)}, f32[1,392,256]{2,1,0:T(8,128)S(1)}, f32[4,200,256]{2,1,0:T(8,128)S(1)}, f32[4,200,256]{2,1,0:T(8,128)S(1)}) custom-call(s32[1,1,24]{2,1,0:T(1,128)} %rows_in.5, s32[1,1,24]{2,1,0:T(1,128)} %cols_in.5, s32[1,1]{1,0:T(1,128)S(6)} %copy.12.live, ...), custom_call_target="tpu_custom_call", output_to_operand_aliasing={{0}: (5, {})} | custom-call | flops 603979776 | bytes 8388608 | tf_op jit(solution)/shard_map/pallas_call | solution.py:231
  25.4 0.9 %collective-permute-done.5 = f16[392,256]{1,0:T(8,128)(2,1)S(1)} collective-permute-done((f16[392,256]{1,0:T(8,128)(2,1)S(1)}, f16[392,256]{1,0:T(8,128)(2,1)S(1)}, u32[]{:S(2)}, u32[]{:S(2)}) %collective-permute-start.5) | collective-permute-done | bytes 200736 | tf_op jit(solution)/shard_map/ppermute | solution.py:253
  26.3 0.0 collective-permute-start.7
  26.4 0.1 fusion
  26.5 2.1 %collective-permute-start.8 = (f16[392,256]{1,0:T(8,128)(2,1)S(1)}, f16[392,256]{1,0:T(8,128)(2,1)S(1)}, u32[]{:S(2)}, u32[]{:S(2)}) collective-permute-start(f16[392,256]{1,0:T(8,128)(2,1)S(1)} %fusion), channel_id=1, source_target_pairs={{0,16},{8,24},{16,0},{24,8},{1,17},{9,25},{17,1},{25,9},{2,18},{10... | collective-permute-start | bytes 602120 | tf_op jit(solution)/shard_map/ppermute | solution.py:253
  28.6 0.1 collective-permute-done.7
  28.7 0.1 add.21
  28.8 0.0 copy-start
  28.8 0.0 copy-start.1
  28.8 1.8 %collective-permute-start.9 = (f16[392,256]{1,0:T(8,128)(2,1)S(1)}, f16[392,256]{1,0:T(8,128)(2,1)S(1)}, u32[]{:S(2)}, u32[]{:S(2)}) collective-permute-start(f16[392,256]{1,0:T(8,128)(2,1)S(1)} %fusion.4), channel_id=1, source_target_pairs={{0,8},{8,0},{16,24},{24,16},{1,9},{9,1},{17,25},{25,17},{2,10},{10... | collective-permute-start | bytes 602120 | tf_op jit(solution)/shard_map/ppermute | solution.py:253
  30.6 0.1 fusion.8
  30.6 1.6 %collective-permute-start.12 = (f16[200,256]{1,0:T(8,128)(2,1)S(1)}, f16[200,256]{1,0:T(8,128)(2,1)S(1)}, u32[]{:S(2)}, u32[]{:S(2)}) collective-permute-start(f16[200,256]{1,0:T(8,128)(2,1)S(1)} %get-tuple-element.46), channel_id=1, source_target_pairs={{0,2},{1,3},{2,0},{3,1},{4,6},{5,7},{6,4},{7,5},{8,10},{9,11},{10,... | collective-permute-start | bytes 307208 | tf_op jit(solution)/shard_map/ppermute | solution.py:256
  32.2 1.5 %collective-permute-start.11 = (f16[200,256]{1,0:T(8,128)(2,1)S(1)}, f16[200,256]{1,0:T(8,128)(2,1)S(1)}, u32[]{:S(2)}, u32[]{:S(2)}) collective-permute-start(f16[200,256]{1,0:T(8,128)(2,1)S(1)} %get-tuple-element.47), channel_id=1, source_target_pairs={{0,4},{1,5},{2,6},{3,7},{4,0},{5,1},{6,2},{7,3},{8,12},{9,13},{10,... | collective-permute-start | bytes 307208 | tf_op jit(solution)/shard_map/ppermute | solution.py:256
  33.7 0.5 %collective-permute-start.10 = (f16[200,256]{1,0:T(8,128)(2,1)S(1)}, f16[200,256]{1,0:T(8,128)(2,1)S(1)}, u32[]{:S(2)}, u32[]{:S(2)}) collective-permute-start(f16[200,256]{1,0:T(8,128)(2,1)S(1)} %get-tuple-element.48), channel_id=1, source_target_pairs={{0,6},{1,7},{2,4},{3,5},{4,2},{5,3},{6,0},{7,1},{8,14},{9,15},{10,... | collective-permute-start | bytes 307208 | tf_op jit(solution)/shard_map/ppermute | solution.py:256
  34.2 5.0 %collective-permute-done.8 = f16[392,256]{1,0:T(8,128)(2,1)S(1)} collective-permute-done((f16[392,256]{1,0:T(8,128)(2,1)S(1)}, f16[392,256]{1,0:T(8,128)(2,1)S(1)}, u32[]{:S(2)}, u32[]{:S(2)}) %collective-permute-start.8) | collective-permute-done | bytes 200736 | tf_op jit(solution)/shard_map/ppermute | solution.py:253
  39.1 0.0 collective-permute-done.9
  39.1 0.1 fusion.1.h_total
  39.2 0.0 collective-permute-done.12
  39.2 0.0 collective-permute-done.11
  39.3 0.0 collective-permute-done.10
  39.3 0.1 fusion.3.w_total
  39.3 0.0 copy-done
  39.3 0.0 copy-done.1
  39.3 0.8 %shard_map.80 = (bf16[192,256]{1,0:T(8,128)(2,1)}, bf16[384,256]{1,0:T(8,128)(2,1)}) custom-call(bf16[192,256]{1,0:T(8,128)(2,1)S(1)} %copy-done, bf16[384,256]{1,0:T(8,128)(2,1)S(1)} %copy-done.1, f32[200,256]{1,0:T(8,128)S(1)} %fusion.3.w_total, f32[392,256]{1,0:T(8,128)S(1)} %fusion.1.h_total), custom_call_target="tpu_custom_call" | custom-call | tf_op jit(solution)/shard_map/pallas_call | solution.py:201
  (2 shorter events, 0.1 us)
Async XLA Ops:
  0.6 9.3 %collective-permute-start = (bf16[192,256]{1,0:T(8,128)(2,1)}, bf16[192,256]{1,0:T(8,128)(2,1)S(1)}, u32[]{:S(2)}, u32[]{:S(2)}) collective-permute-start(bf16[192,256]{1,0:T(8,128)(2,1)} %w_factor.1), channel_id=1, source_target_pairs={{0,2},{1,3},{2,0},{3,1},{4,6},{5,7},{6,4},{7,5},{8,10},{9,11},{10,... | collective-permute-start | bytes 294920 | tf_op jit(solution)/shard_map/ppermute | solution.py:256
  3.6 6.3 %collective-permute-start.1 = (bf16[192,256]{1,0:T(8,128)(2,1)}, bf16[192,256]{1,0:T(8,128)(2,1)S(1)}, u32[]{:S(2)}, u32[]{:S(2)}) collective-permute-start(bf16[192,256]{1,0:T(8,128)(2,1)} %w_factor.1), channel_id=1, source_target_pairs={{0,4},{1,5},{2,6},{3,7},{4,0},{5,1},{6,2},{7,3},{8,12},{9,13},{10,... | collective-permute-start | bytes 294920 | tf_op jit(solution)/shard_map/ppermute | solution.py:256
  5.2 5.7 %collective-permute-start.2 = (bf16[192,256]{1,0:T(8,128)(2,1)}, bf16[192,256]{1,0:T(8,128)(2,1)S(1)}, u32[]{:S(2)}, u32[]{:S(2)}) collective-permute-start(bf16[192,256]{1,0:T(8,128)(2,1)} %w_factor.1), channel_id=1, source_target_pairs={{0,6},{1,7},{2,4},{3,5},{4,2},{5,3},{6,0},{7,1},{8,14},{9,15},{10,... | collective-permute-start | bytes 294920 | tf_op jit(solution)/shard_map/ppermute | solution.py:256
  5.2 10.1 %collective-permute-start.3 = (bf16[384,256]{1,0:T(8,128)(2,1)}, bf16[384,256]{1,0:T(8,128)(2,1)S(1)}, u32[]{:S(2)}, u32[]{:S(2)}) collective-permute-start(bf16[384,256]{1,0:T(8,128)(2,1)} %h_factor.1), channel_id=1, source_target_pairs={{0,24},{8,16},{16,8},{24,0},{1,25},{9,17},{17,9},{25,1},{2,26},{10... | collective-permute-start | bytes 589832 | tf_op jit(solution)/shard_map/ppermute | solution.py:253
  9.9 10.2 %collective-permute-start.4 = (bf16[384,256]{1,0:T(8,128)(2,1)}, bf16[384,256]{1,0:T(8,128)(2,1)S(1)}, u32[]{:S(2)}, u32[]{:S(2)}) collective-permute-start(bf16[384,256]{1,0:T(8,128)(2,1)} %h_factor.1), channel_id=1, source_target_pairs={{0,8},{8,0},{16,24},{24,16},{1,9},{9,1},{17,25},{25,17},{2,10},{10... | collective-permute-start | bytes 589832 | tf_op jit(solution)/shard_map/ppermute | solution.py:253
  15.3 7.5 %collective-permute-start.6 = (bf16[384,256]{1,0:T(8,128)(2,1)S(1)}, bf16[384,256]{1,0:T(8,128)(2,1)S(1)}, u32[]{:S(2)}, u32[]{:S(2)}) collective-permute-start(bf16[384,256]{1,0:T(8,128)(2,1)S(1)} %collective-permute-done.3.refs_0_), channel_id=1, source_target_pairs={{0,8},{8,0},{16,24},{24,16},{1,9},{9,1},{17,25},{25,17},{2,10},{10... | collective-permute-start | bytes 589832 | tf_op jit(solution)/shard_map/ppermute | solution.py:253
  19.3 7.0 %collective-permute-start.5 = (f16[392,256]{1,0:T(8,128)(2,1)S(1)}, f16[392,256]{1,0:T(8,128)(2,1)S(1)}, u32[]{:S(2)}, u32[]{:S(2)}) collective-permute-start(f16[392,256]{1,0:T(8,128)(2,1)S(1)} %fusion.5), channel_id=1, source_target_pairs={{0,8},{8,0},{16,24},{24,16},{1,9},{9,1},{17,25},{25,17},{2,10},{10... | collective-permute-start | bytes 602120 | tf_op jit(solution)/shard_map/ppermute | solution.py:253
  26.3 2.3 %collective-permute-start.7 = (f32[4,200,256]{2,1,0:T(8,128)S(1)}, f32[4,200,256]{2,1,0:T(8,128)S(1)}, u32[]{:S(2)}, u32[]{:S(2)}) collective-permute-start(f32[4,200,256]{2,1,0:T(8,128)S(1)} %get-tuple-element.37), channel_id=1, source_target_pairs={{0,1},{1,0},{2,3},{3,2},{4,5},{5,4},{6,7},{7,6},{8,9},{9,8},{10,11... | collective-permute-start | bytes 2457608 | tf_op jit(solution)/shard_map/ppermute | solution.py:256
  26.5 12.7 %collective-permute-start.8 = (f16[392,256]{1,0:T(8,128)(2,1)S(1)}, f16[392,256]{1,0:T(8,128)(2,1)S(1)}, u32[]{:S(2)}, u32[]{:S(2)}) collective-permute-start(f16[392,256]{1,0:T(8,128)(2,1)S(1)} %fusion), channel_id=1, source_target_pairs={{0,16},{8,24},{16,0},{24,8},{1,17},{9,25},{17,1},{25,9},{2,18},{10... | collective-permute-start | bytes 602120 | tf_op jit(solution)/shard_map/ppermute | solution.py:253
  28.8 10.6 %copy-start = (bf16[192,256]{1,0:T(8,128)(2,1)S(1)}, bf16[192,256]{1,0:T(8,128)(2,1)}, u32[]{:S(2)}) copy-start(bf16[192,256]{1,0:T(8,128)(2,1)} %w_factor.1) | copy-start | bytes 294916
  28.8 10.6 %copy-start.1 = (bf16[384,256]{1,0:T(8,128)(2,1)S(1)}, bf16[384,256]{1,0:T(8,128)(2,1)}, u32[]{:S(2)}) copy-start(bf16[384,256]{1,0:T(8,128)(2,1)} %h_factor.1) | copy-start | bytes 589828
  28.8 10.3 %collective-permute-start.9 = (f16[392,256]{1,0:T(8,128)(2,1)S(1)}, f16[392,256]{1,0:T(8,128)(2,1)S(1)}, u32[]{:S(2)}, u32[]{:S(2)}) collective-permute-start(f16[392,256]{1,0:T(8,128)(2,1)S(1)} %fusion.4), channel_id=1, source_target_pairs={{0,8},{8,0},{16,24},{24,16},{1,9},{9,1},{17,25},{25,17},{2,10},{10... | collective-permute-start | bytes 602120 | tf_op jit(solution)/shard_map/ppermute | solution.py:253
  30.6 8.6 %collective-permute-start.12 = (f16[200,256]{1,0:T(8,128)(2,1)S(1)}, f16[200,256]{1,0:T(8,128)(2,1)S(1)}, u32[]{:S(2)}, u32[]{:S(2)}) collective-permute-start(f16[200,256]{1,0:T(8,128)(2,1)S(1)} %get-tuple-element.46), channel_id=1, source_target_pairs={{0,2},{1,3},{2,0},{3,1},{4,6},{5,7},{6,4},{7,5},{8,10},{9,11},{10,... | collective-permute-start | bytes 307208 | tf_op jit(solution)/shard_map/ppermute | solution.py:256
  32.2 7.1 %collective-permute-start.11 = (f16[200,256]{1,0:T(8,128)(2,1)S(1)}, f16[200,256]{1,0:T(8,128)(2,1)S(1)}, u32[]{:S(2)}, u32[]{:S(2)}) collective-permute-start(f16[200,256]{1,0:T(8,128)(2,1)S(1)} %get-tuple-element.47), channel_id=1, source_target_pairs={{0,4},{1,5},{2,6},{3,7},{4,0},{5,1},{6,2},{7,3},{8,12},{9,13},{10,... | collective-permute-start | bytes 307208 | tf_op jit(solution)/shard_map/ppermute | solution.py:256
  33.7 5.6 %collective-permute-start.10 = (f16[200,256]{1,0:T(8,128)(2,1)S(1)}, f16[200,256]{1,0:T(8,128)(2,1)S(1)}, u32[]{:S(2)}, u32[]{:S(2)}) collective-permute-start(f16[200,256]{1,0:T(8,128)(2,1)S(1)} %get-tuple-element.48), channel_id=1, source_target_pairs={{0,6},{1,7},{2,4},{3,5},{4,2},{5,3},{6,0},{7,1},{8,14},{9,15},{10,... | collective-permute-start | bytes 307208 | tf_op jit(solution)/shard_map/ppermute | solution.py:256

commit v4 on v2

--- a/solution.py
+++ b/solution.py
@@ -189,20 +189,33 @@
             w_outs[i][o, w_rows:, :] = acc[w_len:, :]
 
 
-def finish_kernel(w_factor, h_factor, w_total, h_total, w_next, h_next):
-    for factor, total, out in ((h_factor, h_total, h_next), (w_factor, w_total, w_next)):
+def finish_kernel(w_factor, h_factor, w_total, h_total, w_next, h_next, w_out, h_out, sems):
+    copies = []
+    for factor, total, out, target in (
+        (h_factor, h_total, h_out, h_next),
+        (w_factor, w_total, w_out, w_next),
+    ):
         rows = factor.shape[0]
         denom = jnp.sum(total[rows:, :], axis=0, keepdims=True)
         out[...] = (factor[...].astype(jnp.float32) * total[:rows, :] / denom).astype(out.dtype)
+        copies.append(pltpu.make_async_copy(out, target, sems.at[len(copies)]))
+        copies[-1].start()
+    for copy in copies:
+        copy.wait()
 
 
 def finish(w_factor, h_factor, w_total, h_total):
     vmem = pl.BlockSpec(memory_space=pltpu.VMEM)
+    factors = (w_factor, h_factor)
     return pl.pallas_call(
         finish_kernel,
-        out_shape=[jax.ShapeDtypeStruct(x.shape, x.dtype) for x in (w_factor, h_factor)],
+        out_shape=[jax.ShapeDtypeStruct(x.shape, x.dtype) for x in factors],
         in_specs=[vmem] * 4,
-        out_specs=[vmem] * 2,
+        out_specs=[pl.BlockSpec(memory_space=pl.ANY)] * 2,
+        scratch_shapes=[
+            *[pltpu.VMEM(x.shape, x.dtype) for x in factors],
+            pltpu.SemaphoreType.DMA((2,)),
+        ],
         compiler_params=pltpu.CompilerParams(vmem_limit_bytes=16 * 1024 * 1024),
     )(w_factor, h_factor, w_total, h_total)
 
@@ -324,7 +337,8 @@
 
     w_scale = SCALE / inner_w
     w_got = [send_w(w_outs[i], 0, i) for i in range(1, inner_w)]
-    near, *w_got = lax.optimization_barrier(((terms[1] * h_scale).astype(jnp.float16), *w_got))
+    near = (terms[1][:quarter] * h_scale).astype(jnp.float16)
+    near, *w_got = lax.optimization_barrier((near, *w_got))
     near = send_h(near, 1)
     w_terms = w_outs[0]
     for got in w_got:
@@ -333,6 +347,7 @@
         send_w((w_terms[o] * w_scale).astype(jnp.float16), o) for o in range(1, OUTER)
     ]
 
+    near = jnp.concatenate([near, far[quarter:]])
     h_total = terms[0] * h_scale + across.astype(jnp.float32) + near.astype(jnp.float32)
     if inner_h > 1:
         me_i = lax.rem(lax.axis_index("doc"), inner_h)

time: 40.3 us -> 40.4 us (level)
  transfers between devices with their start and end apart: 13 -> 13, of which waited for: 7 -> 7; matrix products, arithmetic and copies ran while one was open for 3% -> 3% of each run, Pallas kernels for 15% -> 14%
where the time goes in v4:
time: 40.4 us; the launch traced here: 40.2 us
  starting transfers between devices  18.6 us (46%)
  waiting for transfers between devices  9.81 us (24%)
  Pallas kernels  6.45 us (16%)
  blocking collectives  2.37 us (6%)
  between operations  1.44 us (4%)
  other arithmetic  1.43 us (4%)
    ppermute x6, starting transfers between devices, send_h(): return lax.ppermute(x, 'doc', partner(OUTER, inner_h, by_outer, by_inner))  10.5 us
    ppermute x6, waiting for transfers between devices, send_h(): return lax.ppermute(x, 'doc', partner(OUTER, inner_h, by_outer, by_inner))  8.46 us
    ppermute x7, starting transfers between devices, send_w(): return lax.ppermute(x, 'gram', partner(OUTER, inner_w, by_outer, by_inner))  8.1 us
    pallas_call x3, Pallas kernels, run_kernel(): pl.pallas_call(functools.partial(kernel, group, side, inner), out_shape=o...  5.67 us
    all_gather x1, blocking collectives, body(): w_pieces = lax.all_gather(w_outer, 'gram', axis_index_groups=pairs)  2.37 us
    ppermute x7, waiting for transfers between devices, send_w(): return lax.ppermute(x, 'gram', partner(OUTER, inner_w, by_outer, by_inner))  1.35 us
    another operation x1, other arithmetic, body(): w_outer = jnp.stack([w_factor] + w_got)  0.94 us
  transfers between devices with their start and end apart: 13, of which 7 were waited for; matrix products, arithmetic and copies ran while one was open for 3% of the time, Pallas kernels for 14%

profile of v4, /device:TPU:0, one launch (start us, length us, event | category | flops | bytes accessed | tf_op | source)
XLA Modules:
  0.0 40.2 jit_solution(15492324362965222711)
XLA Ops:
  0.6 3.0 %collective-permute-start = (bf16[192,256]{1,0:T(8,128)(2,1)}, bf16[192,256]{1,0:T(8,128)(2,1)S(1)}, u32[]{:S(2)}, u32[]{:S(2)}) collective-permute-start(bf16[192,256]{1,0:T(8,128)(2,1)} %w_factor.1), channel_id=1, source_target_pairs={{0,2},{1,3},{2,0},{3,1},{4,6},{5,7},{6,4},{7,5},{8,10},{9,11},{10,... | collective-permute-start | bytes 294920 | tf_op jit(solution)/shard_map/ppermute | solution.py:269
  3.6 1.5 %collective-permute-start.2 = (bf16[192,256]{1,0:T(8,128)(2,1)}, bf16[192,256]{1,0:T(8,128)(2,1)S(1)}, u32[]{:S(2)}, u32[]{:S(2)}) collective-permute-start(bf16[192,256]{1,0:T(8,128)(2,1)} %w_factor.1), channel_id=1, source_target_pairs={{0,6},{1,7},{2,4},{3,5},{4,2},{5,3},{6,0},{7,1},{8,14},{9,15},{10,... | collective-permute-start | bytes 294920 | tf_op jit(solution)/shard_map/ppermute | solution.py:269
  5.1 0.1 collective-permute-start.1
  5.2 4.1 %collective-permute-start.3 = (bf16[384,256]{1,0:T(8,128)(2,1)}, bf16[384,256]{1,0:T(8,128)(2,1)S(1)}, u32[]{:S(2)}, u32[]{:S(2)}) collective-permute-start(bf16[384,256]{1,0:T(8,128)(2,1)} %h_factor.1), channel_id=1, source_target_pairs={{0,24},{8,16},{16,8},{24,0},{1,25},{9,17},{17,9},{25,1},{2,26},{10... | collective-permute-start | bytes 589832 | tf_op jit(solution)/shard_map/ppermute | solution.py:266
  9.9 0.0 collective-permute-done
  9.9 0.1 collective-permute-start.5
  10.0 0.2 collective-permute-done.2
  10.1 1.1 %collective-permute-done.1 = bf16[192,256]{1,0:T(8,128)(2,1)S(1)} collective-permute-done((bf16[192,256]{1,0:T(8,128)(2,1)}, bf16[192,256]{1,0:T(8,128)(2,1)S(1)}, u32[]{:S(2)}, u32[]{:S(2)}) %collective-permute-start.1) | collective-permute-done | bytes 98336 | tf_op jit(solution)/shard_map/ppermute | solution.py:269
  11.3 0.9 %pad_maximum_fusion = bf16[4,192,256]{2,1,0:T(8,128)(2,1)S(1)} fusion(bf16[1,192,256]{2,1,0:T(8,128)(2,1)S(1)} %bitcast.34, bf16[1,192,256]{2,1,0:T(8,128)(2,1)S(1)} %bitcast.35, bf16[1,192,256]{2,1,0:T(8,128)(2,1)S(1)} %bitcast.33, bf16[1,192,256]{2,1,0:T(8,128)(2,1)} %bitcast.32), kind=kLoop, calls=%fused_computation.5 | loop fusion | flops 589824 | bytes 786432 | tf_op jit(solution)/shard_map/stack | solution.py:283
  12.2 2.4 %all-gather = bf16[8,192,256]{2,1,0:T(8,128)(2,1)S(1)} all-gather(bf16[4,192,256]{2,1,0:T(8,128)(2,1)S(1)} %pad_maximum_fusion), channel_id=2, replica_groups={{0,1},{2,3},{4,5},{6,7},{8,9},{10,11},{12,13},{14,15},{16,17},{18,19},{..., dimensions={0}, use_global_device_ids=true | all-gather | bytes 1179648 | tf_op jit(solution)/shard_map/all_gather | solution.py:285
  14.6 0.7 %collective-permute-done.3.refs_0_ = bf16[384,256]{1,0:T(8,128)(2,1)S(1)} collective-permute-done((bf16[384,256]{1,0:T(8,128)(2,1)}, bf16[384,256]{1,0:T(8,128)(2,1)S(1)}, u32[]{:S(2)}, u32[]{:S(2)}) %collective-permute-start.3) | collective-permute-done | bytes 196640 | tf_op jit(solution)/shard_map/ppermute | solution.py:266
  15.3 2.2 %collective-permute-start.6 = (bf16[384,256]{1,0:T(8,128)(2,1)S(1)}, bf16[384,256]{1,0:T(8,128)(2,1)S(1)}, u32[]{:S(2)}, u32[]{:S(2)}) collective-permute-start(bf16[384,256]{1,0:T(8,128)(2,1)S(1)} %collective-permute-done.3.refs_0_), channel_id=1, source_target_pairs={{0,8},{8,0},{16,24},{24,16},{1,9},{9,1},{17,25},{25,17},{2,10},{10... | collective-permute-start | bytes 589832 | tf_op jit(solution)/shard_map/ppermute | solution.py:266
  17.4 1.8 %shard_map.77 = (bf16[1536,256]{1,0:T(8,128)(2,1)S(1)}, f32[1544,256]{1,0:T(8,128)S(1)}, bf16[24,128,128]{2,1,0:T(8,128)(2,1)S(1)}, f32[8,256]{1,0:T(8,128)S(1)}, f32[1,392,256]{2,1,0:T(8,128)S(1)}) custom-call(s32[1,1,24]{2,1,0:T(1,128)} %rows_in.5, s32[1,1,24]{2,1,0:T(1,128)} %cols_in.5, s32[1,1]{1,0:T(1,128)S(6)} %copy.12.live, ...), custom_call_target="tpu_custom_call" | custom-call | flops 150994944 | bytes 8388608 | tf_op jit(solution)/shard_map/pallas_call | solution.py:244
  19.3 0.4 collective-permute-start.4
  19.7 0.0 collective-permute-done.5.refs_1_
  19.7 2.1 %shard_map.78 = (f32[1544,256]{1,0:T(8,128)S(1)}, f32[2,392,256]{2,1,0:T(8,128)S(1)}) custom-call(s32[1,1,24]{2,1,0:T(1,128)} %rows_in.5, s32[1,1,24]{2,1,0:T(1,128)} %cols_in.5, s32[1,1]{1,0:T(1,128)S(6)} %copy.12.live, bf16[24,128,128]{2,1,0:T(8,128)(2,1)S(1)} %get-tuple-element.25.counts, ...), custom_call_target="tpu_custom_call", output_to_operand_aliasing={{0}: (5, {})} | custom-call | flops 301989888 | bytes 8388608 | tf_op jit(solution)/shard_map/pallas_call | solution.py:244
  21.8 1.4 %collective-permute-done.6.refs_0_ = bf16[384,256]{1,0:T(8,128)(2,1)S(1)} collective-permute-done((bf16[384,256]{1,0:T(8,128)(2,1)S(1)}, bf16[384,256]{1,0:T(8,128)(2,1)S(1)}, u32[]{:S(2)}, u32[]{:S(2)}) %collective-permute-start.6) | collective-permute-done | bytes 196640 | tf_op jit(solution)/shard_map/ppermute | solution.py:266
  23.2 1.7 %shard_map.79 = (f32[1544,256]{1,0:T(8,128)S(1)}, f32[1,392,256]{2,1,0:T(8,128)S(1)}, f32[4,200,256]{2,1,0:T(8,128)S(1)}, f32[4,200,256]{2,1,0:T(8,128)S(1)}) custom-call(s32[1,1,24]{2,1,0:T(1,128)} %rows_in.5, s32[1,1,24]{2,1,0:T(1,128)} %cols_in.5, s32[1,1]{1,0:T(1,128)S(6)} %copy.12.live, ...), custom_call_target="tpu_custom_call", output_to_operand_aliasing={{0}: (5, {})} | custom-call | flops 150994944 | bytes 8388608 | tf_op jit(solution)/shard_map/pallas_call | solution.py:244
  25.0 1.3 %collective-permute-done.4 = f16[392,256]{1,0:T(8,128)(2,1)S(1)} collective-permute-done((f16[392,256]{1,0:T(8,128)(2,1)S(1)}, f16[392,256]{1,0:T(8,128)(2,1)S(1)}, u32[]{:S(2)}, u32[]{:S(2)}) %collective-permute-start.4) | collective-permute-done | bytes 200736 | tf_op jit(solution)/shard_map/ppermute | solution.py:266
  26.3 0.0 collective-permute-start.7
  26.4 0.1 fusion
  26.5 2.1 %collective-permute-start.8 = (f16[392,256]{1,0:T(8,128)(2,1)S(1)}, f16[392,256]{1,0:T(8,128)(2,1)S(1)}, u32[]{:S(2)}, u32[]{:S(2)}) collective-permute-start(f16[392,256]{1,0:T(8,128)(2,1)S(1)} %fusion), channel_id=1, source_target_pairs={{0,16},{8,24},{16,0},{24,8},{1,17},{9,25},{17,1},{25,9},{2,18},{10... | collective-permute-start | bytes 602120 | tf_op jit(solution)/shard_map/ppermute | solution.py:266
  28.6 0.1 collective-permute-done.7
  28.7 1.7 %collective-permute-start.9 = (f16[384,256]{1,0:T(8,128)(2,1)S(1)}, f16[384,256]{1,0:T(8,128)(2,1)S(1)}, u32[]{:S(2)}, u32[]{:S(2)}) collective-permute-start(f16[384,256]{1,0:T(8,128)(2,1)S(1)} %fusion.10), channel_id=1, source_target_pairs={{0,8},{8,0},{16,24},{24,16},{1,9},{9,1},{17,25},{25,17},{2,10},{10... | collective-permute-start | bytes 589832 | tf_op jit(solution)/shard_map/ppermute | solution.py:266
  30.4 0.1 add.21
  30.5 0.0 copy-start
  30.5 0.0 copy-start.1
  30.5 0.1 fusion.13
  30.6 1.6 %collective-permute-start.10 = (f16[200,256]{1,0:T(8,128)(2,1)S(1)}, f16[200,256]{1,0:T(8,128)(2,1)S(1)}, u32[]{:S(2)}, u32[]{:S(2)}) collective-permute-start(f16[200,256]{1,0:T(8,128)(2,1)S(1)} %get-tuple-element.46), channel_id=1, source_target_pairs={{0,2},{1,3},{2,0},{3,1},{4,6},{5,7},{6,4},{7,5},{8,10},{9,11},{10,... | collective-permute-start | bytes 307208 | tf_op jit(solution)/shard_map/ppermute | solution.py:269
  32.1 1.5 %collective-permute-start.11 = (f16[200,256]{1,0:T(8,128)(2,1)S(1)}, f16[200,256]{1,0:T(8,128)(2,1)S(1)}, u32[]{:S(2)}, u32[]{:S(2)}) collective-permute-start(f16[200,256]{1,0:T(8,128)(2,1)S(1)} %get-tuple-element.45), channel_id=1, source_target_pairs={{0,4},{1,5},{2,6},{3,7},{4,0},{5,1},{6,2},{7,3},{8,12},{9,13},{10,... | collective-permute-start | bytes 307208 | tf_op jit(solution)/shard_map/ppermute | solution.py:269
  33.6 0.5 %collective-permute-start.12 = (f16[200,256]{1,0:T(8,128)(2,1)S(1)}, f16[200,256]{1,0:T(8,128)(2,1)S(1)}, u32[]{:S(2)}, u32[]{:S(2)}) collective-permute-start(f16[200,256]{1,0:T(8,128)(2,1)S(1)} %get-tuple-element.44), channel_id=1, source_target_pairs={{0,6},{1,7},{2,4},{3,5},{4,2},{5,3},{6,0},{7,1},{8,14},{9,15},{10,... | collective-permute-start | bytes 307208 | tf_op jit(solution)/shard_map/ppermute | solution.py:269
  34.1 5.0 %collective-permute-done.8 = f16[392,256]{1,0:T(8,128)(2,1)S(1)} collective-permute-done((f16[392,256]{1,0:T(8,128)(2,1)S(1)}, f16[392,256]{1,0:T(8,128)(2,1)S(1)}, u32[]{:S(2)}, u32[]{:S(2)}) %collective-permute-start.8) | collective-permute-done | bytes 200736 | tf_op jit(solution)/shard_map/ppermute | solution.py:266
  39.1 0.0 collective-permute-done.9
  39.1 0.1 fusion.1.h_total
  39.2 0.0 collective-permute-done.10
  39.2 0.0 collective-permute-done.11
  39.3 0.0 collective-permute-done.12
  39.3 0.1 fusion.8.w_total
  39.4 0.0 copy-done
  39.4 0.0 copy-done.1
  39.4 0.8 %shard_map.80 = (bf16[192,256]{1,0:T(8,128)(2,1)}, bf16[384,256]{1,0:T(8,128)(2,1)}) custom-call(bf16[192,256]{1,0:T(8,128)(2,1)S(1)} %copy-done.1, bf16[384,256]{1,0:T(8,128)(2,1)S(1)} %copy-done, f32[200,256]{1,0:T(8,128)S(1)} %fusion.8.w_total, f32[392,256]{1,0:T(8,128)S(1)} %fusion.1.h_total), custom_call_target="tpu_custom_call" | custom-call | tf_op jit(solution)/shard_map/pallas_call | solution.py:210
  (3 shorter events, 0.1 us)
Async XLA Ops:
  0.6 9.3 %collective-permute-start = (bf16[192,256]{1,0:T(8,128)(2,1)}, bf16[192,256]{1,0:T(8,128)(2,1)S(1)}, u32[]{:S(2)}, u32[]{:S(2)}) collective-permute-start(bf16[192,256]{1,0:T(8,128)(2,1)} %w_factor.1), channel_id=1, source_target_pairs={{0,2},{1,3},{2,0},{3,1},{4,6},{5,7},{6,4},{7,5},{8,10},{9,11},{10,... | collective-permute-start | bytes 294920 | tf_op jit(solution)/shard_map/ppermute | solution.py:269
  3.6 6.5 %collective-permute-start.2 = (bf16[192,256]{1,0:T(8,128)(2,1)}, bf16[192,256]{1,0:T(8,128)(2,1)S(1)}, u32[]{:S(2)}, u32[]{:S(2)}) collective-permute-start(bf16[192,256]{1,0:T(8,128)(2,1)} %w_factor.1), channel_id=1, source_target_pairs={{0,6},{1,7},{2,4},{3,5},{4,2},{5,3},{6,0},{7,1},{8,14},{9,15},{10,... | collective-permute-start | bytes 294920 | tf_op jit(solution)/shard_map/ppermute | solution.py:269
  5.1 6.1 %collective-permute-start.1 = (bf16[192,256]{1,0:T(8,128)(2,1)}, bf16[192,256]{1,0:T(8,128)(2,1)S(1)}, u32[]{:S(2)}, u32[]{:S(2)}) collective-permute-start(bf16[192,256]{1,0:T(8,128)(2,1)} %w_factor.1), channel_id=1, source_target_pairs={{0,4},{1,5},{2,6},{3,7},{4,0},{5,1},{6,2},{7,3},{8,12},{9,13},{10,... | collective-permute-start | bytes 294920 | tf_op jit(solution)/shard_map/ppermute | solution.py:269
  5.2 10.1 %collective-permute-start.3 = (bf16[384,256]{1,0:T(8,128)(2,1)}, bf16[384,256]{1,0:T(8,128)(2,1)S(1)}, u32[]{:S(2)}, u32[]{:S(2)}) collective-permute-start(bf16[384,256]{1,0:T(8,128)(2,1)} %h_factor.1), channel_id=1, source_target_pairs={{0,24},{8,16},{16,8},{24,0},{1,25},{9,17},{17,9},{25,1},{2,26},{10... | collective-permute-start | bytes 589832 | tf_op jit(solution)/shard_map/ppermute | solution.py:266
  9.9 9.8 %collective-permute-start.5 = (bf16[384,256]{1,0:T(8,128)(2,1)}, bf16[384,256]{1,0:T(8,128)(2,1)S(1)}, u32[]{:S(2)}, u32[]{:S(2)}) collective-permute-start(bf16[384,256]{1,0:T(8,128)(2,1)} %h_factor.1), channel_id=1, source_target_pairs={{0,8},{8,0},{16,24},{24,16},{1,9},{9,1},{17,25},{25,17},{2,10},{10... | collective-permute-start | bytes 589832 | tf_op jit(solution)/shard_map/ppermute | solution.py:266
  15.3 8.0 %collective-permute-start.6 = (bf16[384,256]{1,0:T(8,128)(2,1)S(1)}, bf16[384,256]{1,0:T(8,128)(2,1)S(1)}, u32[]{:S(2)}, u32[]{:S(2)}) collective-permute-start(bf16[384,256]{1,0:T(8,128)(2,1)S(1)} %collective-permute-done.3.refs_0_), channel_id=1, source_target_pairs={{0,8},{8,0},{16,24},{24,16},{1,9},{9,1},{17,25},{25,17},{2,10},{10... | collective-permute-start | bytes 589832 | tf_op jit(solution)/shard_map/ppermute | solution.py:266
  19.3 7.0 %collective-permute-start.4 = (f16[392,256]{1,0:T(8,128)(2,1)S(1)}, f16[392,256]{1,0:T(8,128)(2,1)S(1)}, u32[]{:S(2)}, u32[]{:S(2)}) collective-permute-start(f16[392,256]{1,0:T(8,128)(2,1)S(1)} %fusion.9), channel_id=1, source_target_pairs={{0,8},{8,0},{16,24},{24,16},{1,9},{9,1},{17,25},{25,17},{2,10},{10... | collective-permute-start | bytes 602120 | tf_op jit(solution)/shard_map/ppermute | solution.py:266
  26.3 2.3 %collective-permute-start.7 = (f32[4,200,256]{2,1,0:T(8,128)S(1)}, f32[4,200,256]{2,1,0:T(8,128)S(1)}, u32[]{:S(2)}, u32[]{:S(2)}) collective-permute-start(f32[4,200,256]{2,1,0:T(8,128)S(1)} %get-tuple-element.35), channel_id=1, source_target_pairs={{0,1},{1,0},{2,3},{3,2},{4,5},{5,4},{6,7},{7,6},{8,9},{9,8},{10,11... | collective-permute-start | bytes 2457608 | tf_op jit(solution)/shard_map/ppermute | solution.py:269
  26.5 12.7 %collective-permute-start.8 = (f16[392,256]{1,0:T(8,128)(2,1)S(1)}, f16[392,256]{1,0:T(8,128)(2,1)S(1)}, u32[]{:S(2)}, u32[]{:S(2)}) collective-permute-start(f16[392,256]{1,0:T(8,128)(2,1)S(1)} %fusion), channel_id=1, source_target_pairs={{0,16},{8,24},{16,0},{24,8},{1,17},{9,25},{17,1},{25,9},{2,18},{10... | collective-permute-start | bytes 602120 | tf_op jit(solution)/shard_map/ppermute | solution.py:266
  28.7 10.5 %collective-permute-start.9 = (f16[384,256]{1,0:T(8,128)(2,1)S(1)}, f16[384,256]{1,0:T(8,128)(2,1)S(1)}, u32[]{:S(2)}, u32[]{:S(2)}) collective-permute-start(f16[384,256]{1,0:T(8,128)(2,1)S(1)} %fusion.10), channel_id=1, source_target_pairs={{0,8},{8,0},{16,24},{24,16},{1,9},{9,1},{17,25},{25,17},{2,10},{10... | collective-permute-start | bytes 589832 | tf_op jit(solution)/shard_map/ppermute | solution.py:266
  30.5 8.9 %copy-start = (bf16[384,256]{1,0:T(8,128)(2,1)S(1)}, bf16[384,256]{1,0:T(8,128)(2,1)}, u32[]{:S(2)}) copy-start(bf16[384,256]{1,0:T(8,128)(2,1)} %h_factor.1) | copy-start | bytes 589828
  30.5 8.9 %copy-start.1 = (bf16[192,256]{1,0:T(8,128)(2,1)S(1)}, bf16[192,256]{1,0:T(8,128)(2,1)}, u32[]{:S(2)}) copy-start(bf16[192,256]{1,0:T(8,128)(2,1)} %w_factor.1) | copy-start | bytes 294916
  30.6 8.7 %collective-permute-start.10 = (f16[200,256]{1,0:T(8,128)(2,1)S(1)}, f16[200,256]{1,0:T(8,128)(2,1)S(1)}, u32[]{:S(2)}, u32[]{:S(2)}) collective-permute-start(f16[200,256]{1,0:T(8,128)(2,1)S(1)} %get-tuple-element.46), channel_id=1, source_target_pairs={{0,2},{1,3},{2,0},{3,1},{4,6},{5,7},{6,4},{7,5},{8,10},{9,11},{10,... | collective-permute-start | bytes 307208 | tf_op jit(solution)/shard_map/ppermute | solution.py:269
  32.1 7.1 %collective-permute-start.11 = (f16[200,256]{1,0:T(8,128)(2,1)S(1)}, f16[200,256]{1,0:T(8,128)(2,1)S(1)}, u32[]{:S(2)}, u32[]{:S(2)}) collective-permute-start(f16[200,256]{1,0:T(8,128)(2,1)S(1)} %get-tuple-element.45), channel_id=1, source_target_pairs={{0,4},{1,5},{2,6},{3,7},{4,0},{5,1},{6,2},{7,3},{8,12},{9,13},{10,... | collective-permute-start | bytes 307208 | tf_op jit(solution)/shard_map/ppermute | solution.py:269
  33.6 5.6 %collective-permute-start.12 = (f16[200,256]{1,0:T(8,128)(2,1)S(1)}, f16[200,256]{1,0:T(8,128)(2,1)S(1)}, u32[]{:S(2)}, u32[]{:S(2)}) collective-permute-start(f16[200,256]{1,0:T(8,128)(2,1)S(1)} %get-tuple-element.44), channel_id=1, source_target_pairs={{0,6},{1,7},{2,4},{3,5},{4,2},{5,3},{6,0},{7,1},{8,14},{9,15},{10,... | collective-permute-start | bytes 307208 | tf_op jit(solution)/shard_map/ppermute | solution.py:269
